TPU v7x, 32 devices: a whole 2x2x4 slice. The times are simulated.
32 devices in a mesh: slab: 16 (over z, x, core), ang: 2 (over y).
Axes of the slice: x: 2, y: 2, z: 4, core: 2. Of those that a mesh axis runs over, the one named last changes fastest.
Arguments:
- volume: float32 [128, 256, 4096], P('slab', 'ang'), may hold values from 0.1 to 3
- measured: bfloat16 [8, 512, 4096], P('ang', 'slab'), may hold values from 0 to 2
- foot_start: int32 [16, 8], P('slab', 'ang'), may hold values from 0 to 480, as said below
- foot_len: int32 [16, 8], P('slab', 'ang'), may hold values from 32 to 96
- order: int32 [64], replicated, may hold values from 0 to 63, each once
- ray_table: float32 [64, 256], replicated, may hold values from 0.001953125 to 0.0078125
Outputs:
- updated: float32 [128, 256, 4096], P('slab', 'ang')
- residual: float32 [8, 512, 4096], P('ang', 'slab')
Inputs may be any that keep to these rules, and one draw needn't show every extreme that they name: foot_start[s, j] + foot_len[s, j] <= 512; the footprint of slab s lies within rows (s - 2) * 32 to (s + 3) * 32.
All inputs are finite; a program needn't handle non-finite values.
Results may differ from a plain program's by a relative error of at most 0.0003.
Values sent between devices are 32-bit elements; how exact they have to be, the bound alone decides.
No kernel may reach another device: no remote copies, remote signals or barrier semaphores. Data moves between devices by JAX's collectives and lax.ppermute only.
A program may use at most 128 MiB of HBM per device.

v0:
```python
import jax
import jax.numpy as jnp
from jax import lax
from jax.sharding import PartitionSpec as P

ZDEV = 8
ANGLES = 8


def from_behind(value, axis, steps):
    count = lax.axis_size(axis)
    leading, last = (max(0, -steps), min(count, count - steps))
    return lax.ppermute(value, axis, [(source, source + steps) for source in range(leading, last)])


def with_halo(value, sides, width):
    for axis, dim in sides:
        devices, length = (lax.axis_size(axis), value.shape[dim])
        up = [(i, (i + 1) % devices) for i in range(devices - 1)]
        down = [(j, i) for i, j in up]
        last = lax.slice_in_dim(value, length - width, length, axis=dim)
        leading = lax.slice_in_dim(value, 0, width, axis=dim)
        before = lax.ppermute(last, axis, up)
        after = lax.ppermute(leading, axis, down)
        value = jnp.concatenate([before, value, after], axis=dim)
    return value


def hat_weights(starts, lengths, rows):
    first = starts[..., None, None]
    span_len = lengths[..., None, None]
    span = span_len / ZDEV
    centre = first + (jnp.arange(ZDEV, dtype=jnp.float32)[None, :] + 0.5) * span
    row_pos = rows[:, None]
    weight = jnp.maximum(0.0, 1.0 - jnp.abs(row_pos + 0.5 - centre) / span)
    inside = jnp.logical_and(row_pos >= first, row_pos < first + span_len)
    return jnp.where(inside, weight, 0.0)


def near_sum(blocks, cover_blocks):
    totals = blocks[:, 2]
    cover = cover_blocks[:, 2]
    for offset in (-2, -1, 1, 2):
        moved, moved_cover = from_behind(
            (blocks[:, offset + 2], cover_blocks[:, offset + 2]), "slab", offset
        )
        totals = totals + moved
        cover = cover + moved_cover
    return (totals, cover)


def halo_rows(own_rows):
    rows_dev = own_rows.shape[1]
    inner = own_rows
    result = own_rows
    for turn in range(2):
        if turn == 0:
            source = own_rows
        else:
            source = jnp.concatenate([inner[:, 2 * rows_dev :], inner[:, :rows_dev]], axis=1)
        grown = with_halo(source, (("slab", 1),), rows_dev)
        if turn == 0:
            inner = grown
        else:
            result = jnp.concatenate([grown[:, :rows_dev], inner, grown[:, -rows_dev:]], axis=1)
    return result


def body(volume, measured, foot_start, foot_len, order, ray_table):
    high = lax.Precision.HIGHEST
    slab_pos = lax.axis_index("slab")
    ang_pos = lax.axis_index("ang")
    per_dev = measured.shape[0]
    rows_dev = measured.shape[1]
    share = volume.shape[1]
    picked = order[:ANGLES]
    onehot = (picked[:, None] == jnp.arange(ray_table.shape[0], dtype=jnp.int32)[None, :]).astype(
        jnp.float32
    )
    weights_all = jnp.dot(onehot, ray_table, precision=high)
    weights_mine = lax.dynamic_slice_in_dim(weights_all, ang_pos * per_dev, per_dev, 0)
    path = weights_mine.sum(1)
    weights_cells = lax.dynamic_slice_in_dim(weights_all, ang_pos * share, share, 1)
    ray_part = jnp.einsum("ay,zyx->azx", weights_cells, volume, precision=high)
    summed_all = lax.psum(ray_part, "ang")
    summed = lax.dynamic_slice_in_dim(summed_all, ang_pos * per_dev, per_dev, 0)
    starts = foot_start[0].astype(jnp.float32)
    lengths = foot_len[0].astype(jnp.float32)
    first_row = (slab_pos - 2) * rows_dev
    rows = (first_row + lax.iota(jnp.int32, 5 * rows_dev)).astype(jnp.float32)
    kernel = hat_weights(starts, lengths, rows)
    partial_value = jnp.einsum("arz,azx->arx", kernel, summed, precision=high)
    coverage = kernel.sum(-1)
    blocks = partial_value.reshape(per_dev, 5, rows_dev, partial_value.shape[2])
    cover_blocks = coverage.reshape(per_dev, 5, rows_dev)
    totals, cover = near_sum(blocks, cover_blocks)
    denom = jnp.maximum(path[:, None] * cover, 0.25)
    res_mine = (measured.astype(jnp.float32) - totals) / denom[:, :, None]
    res_rows = halo_rows(res_mine)
    back = jnp.einsum("arz,arx->azx", kernel, res_rows, precision=high)
    slice_weight = kernel.sum(1)
    back_all, slice_all = (
        lax.all_gather(back, "ang", axis=0, tiled=True),
        lax.all_gather(slice_weight, "ang", axis=0, tiled=True),
    )
    update = jnp.einsum("ay,azx->zyx", weights_cells, back_all, precision=high)
    column = jnp.einsum("ay,az->zy", weights_cells, slice_all, precision=high)
    updated = volume + update / column[:, :, None]
    return (updated, res_mine)


def solution(mesh):
    return jax.shard_map(
        body,
        mesh=mesh,
        in_specs=(
            P("slab", "ang", None),
            P("ang", "slab", None),
            P("slab", "ang"),
            P("slab", "ang"),
            P(),
            P(),
        ),
        out_specs=(P("slab", "ang", None), P("ang", "slab", None)),
        check_vma=False,
    )
```

profile of v0, /device:TPU:0, one launch (start us, length us, event | category | flops | bytes accessed | tf_op | source)
XLA Modules:
  0.0 421.6 jit_solution(5903490183505642949)
XLA Ops:
  7.2 0.0 copy-start
  7.2 0.0 all-reduce.2.cloned.1.call-start
  7.2 0.8 copy-done
  8.0 0.8 fusion.15
  8.9 11.5 %fusion.13 = f32[8,8,4096]{2,0,1:T(8,128)} fusion(f32[8,128,4096]{2,1,0:T(8,128)} %param.6, f32[8,256]{1,0:T(8,128)S(1)} %fusion.15, s32[]{:T(128)S(6)} %select_n.12), kind=kOutput, calls=%fused_computation.25 | convolution fusion | flops 402653184 | bytes 17829892 | tf_op jit(solution)/shard_map/ay,zyx->azx/dot_general | solution.py:84
  20.3 0.0 all-reduce.2.cloned.1.call-update
  20.4 0.0 all-gather.3.cloned.1.call-start
  20.5 0.0 copy-done.7
  20.5 0.0 copy-done.6
  20.5 0.1 compare_and_fusion
  20.6 0.1 multiply_add_fusion
  20.6 42.6 %all-reduce.2.cloned.1.call-done = f32[8,8,4096]{2,0,1:T(8,128)} async-done(((f32[8,8,4096]{2,0,1:T(8,128)}), f32[8,8,4096]{2,0,1:T(8,128)}) %all-reduce.2.cloned.1.call-update) | async-done | bytes 1048592 | tf_op jit(solution)/shard_map/psum | solution.py:85
  63.3 1.3 constant_dynamic-slice_fusion
  64.6 8.5 %fusion.7 = f32[4,160,4096]{2,1,0:T(8,128)S(1)} fusion(f32[4,8,4096]{2,0,1:T(4,128)S(1)} %constant_dynamic-slice_fusion, f32[4]{0:T(128)S(1)} %get-tuple-element.20, f32[4,8]{1,0:T(4,128)S(1)} %multiply_add_fusion, f32[160]{0:T(256)S(1)} %broadcast_add_fusion, pred[4,160]{1,0:T(4,128)(4,1)S(1)} %compare_and_fusion), kind=kOutput, calls=%fused_computation.13 | convolution fusion | flops 251688960 | bytes 11011472 | tf_op jit(solution)/shard_map/arz,azx->arx/dot_general | solution.py:92
  73.1 0.0 copy-start.2
  73.1 0.0 copy-start.5
  73.1 3.4 slice_bitcast_fusion.3
  76.6 3.2 copy-done.2
  79.7 1.3 collective-permute-start
  81.0 3.1 collective-permute-start.2
  84.2 1.3 collective-permute-start.1
  85.4 7.1 %collective-permute-start.3 = (f32[4,32,4096]{2,1,0:T(8,128)}, f32[4,32,4096]{2,1,0:T(8,128)}, u32[]{:S(2)}, u32[]{:S(2)}) collective-permute-start(f32[4,32,4096]{2,1,0:T(8,128)} %get-tuple-element.13), channel_id=1, source_target_pairs={{0,4},{2,6},{4,8},{6,10},{8,12},{10,14},{12,16},{14,18},{16,20},{1... | collective-permute-start | bytes 6291464 | tf_op jit(solution)/shard_map/ppermute | solution.py:13
  92.5 0.2 fusion.11
  92.7 0.1 reshape.159
  92.8 3.8 collective-permute-start.7
  96.6 100.1 %collective-permute-done.7 = f32[4,32]{1,0:T(4,128)S(1)} collective-permute-done((f32[4,32]{1,0:T(4,128)S(1)}, f32[4,32]{1,0:T(4,128)S(1)}, u32[]{:S(2)}, u32[]{:S(2)}) %collective-permute-start.7) | collective-permute-done | bytes 544 | tf_op jit(solution)/shard_map/ppermute | solution.py:13
  196.7 1.3 collective-permute-start.4
  198.0 4.6 %collective-permute-done.4 = f32[4,32]{1,0:T(4,128)S(1)} collective-permute-done((f32[4,32]{1,0:T(4,128)S(1)}, f32[4,32]{1,0:T(4,128)S(1)}, u32[]{:S(2)}, u32[]{:S(2)}) %collective-permute-start.4) | collective-permute-done | bytes 544 | tf_op jit(solution)/shard_map/ppermute | solution.py:13
  202.6 23.3 %collective-permute-start.6 = (f32[4,32]{1,0:T(4,128)S(1)}, f32[4,32]{1,0:T(4,128)S(1)}, u32[]{:S(2)}, u32[]{:S(2)}) collective-permute-start(f32[4,32]{1,0:T(4,128)S(1)} %bitcast.65), channel_id=1, source_target_pairs={{0,2},{2,4},{4,6},{6,8},{8,10},{10,12},{12,14},{14,16},{16,18},{18... | collective-permute-start | bytes 1544 | tf_op jit(solution)/shard_map/ppermute | solution.py:13
  225.9 0.8 collective-permute-done.6
  226.7 1.3 collective-permute-start.5
  228.0 0.1 dynamic-slice_reduce_fusion
  228.1 1.6 collective-permute-done.5
  229.7 0.1 multiply_maximum_fusion
  229.8 0.0 collective-permute-done
  229.8 0.0 collective-permute-done.2
  229.8 0.0 collective-permute-done.1
  229.8 1.3 copy-done.4
  231.1 0.0 collective-permute-done.3
  231.1 0.0 copy-done.5
  231.1 5.1 %fusion.5 = f32[4,32,4096]{2,1,0:T(8,128)S(1)} fusion(f32[4,32,4096]{2,1,0:T(8,128)} %collective-permute-done.3, f32[4,32,4096]{2,1,0:T(8,128)} %collective-permute-done.2, f32[4,32,4096]{2,1,0:T(8,128)} %collective-permute-done.1, f32[4,32,4096]{2,1,0:T(8,128)} %copy-done.4, f32[4,5,32,4096]{3,2,1,0:T(8,128)} %bitcast.60, ...), kind=kLoop, calls=%fused_computation.11 | loop fusion | flops 3670016 | bytes 13632000 | tf_op jit(solution)/shard_map/div | solution.py:98
  236.3 0.0 copy-start.3
  236.3 4.9 %collective-permute-start.8 = (f32[4,32,4096]{2,1,0:T(8,128)S(1)}, f32[4,32,4096]{2,1,0:T(8,128)S(1)}, u32[]{:S(2)}, u32[]{:S(2)}) collective-permute-start(f32[4,32,4096]{2,1,0:T(8,128)S(1)} %fusion.5), channel_id=1, source_target_pairs={{0,2},{2,4},{4,6},{6,8},{8,10},{10,12},{12,14},{14,16},{16,18},{18... | collective-permute-start | bytes 6291464 | tf_op jit(solution)/shard_map/ppermute | solution.py:23
  241.2 1.3 collective-permute-start.10
  242.5 2.3 collective-permute-done.8
  244.8 43.7 %collective-permute-start.9 = (f32[4,32,4096]{2,1,0:T(8,128)S(1)}, f32[4,32,4096]{2,1,0:T(8,128)S(1)}, u32[]{:S(2)}, u32[]{:S(2)}) collective-permute-start(f32[4,32,4096]{2,1,0:T(8,128)S(1)} %collective-permute-done.8), channel_id=1, source_target_pairs={{0,2},{2,4},{4,6},{6,8},{8,10},{10,12},{12,14},{14,16},{16,18},{18... | collective-permute-start | bytes 6291464 | tf_op jit(solution)/shard_map/ppermute | solution.py:23
  288.6 0.0 collective-permute-done.10
  288.6 1.3 collective-permute-start.11
  289.9 2.3 collective-permute-done.9
  292.2 0.2 constant_dynamic-update-slice_fusion.4
  292.4 0.2 constant_dynamic-update-slice_fusion.3
  292.6 0.0 copy-done.3
  292.6 0.2 constant_dynamic-update-slice_fusion.2
  292.8 0.2 constant_dynamic-update-slice_fusion.1
  293.0 3.5 collective-permute-done.11
  296.5 0.2 constant_dynamic-update-slice_fusion
  296.7 5.8 %fusion.10 = f32[4,8,4096]{2,1,0:T(8,128)} fusion(f32[4,160,4096]{2,1,0:T(8,128)S(1)} %constant_dynamic-update-slice_fusion, f32[4]{0:T(128)S(1)} %get-tuple-element.20, f32[4,8]{1,0:T(4,128)S(1)} %multiply_add_fusion, f32[160]{0:T(256)S(1)} %broadcast_add_fusion, pred[4,160]{1,0:T(4,128)(4,1)S(1)} %compare_and_fusion), kind=kOutput, calls=%fused_computation.17 | convolution fusion | flops 251688960 | bytes 11011472 | tf_op jit(solution)/shard_map/arz,arx->azx/dot_general | solution.py:100
  302.5 0.0 all-gather.3.cloned.1.call-update
  302.6 17.4 %copy.29 = f32[8,128,4096]{1,2,0:T(8,128)} copy(f32[8,128,4096]{2,1,0:T(8,128)} %param.6) | data formatting | bytes 33554432 | tf_op args[0]
  320.0 4.5 %all-gather = f32[2,4,8]{2,1,0:T(4,128)S(1)} all-gather(f32[1,4,8]{2,1,0:T(4,128)S(1)} %bitcast.63), channel_id=1, replica_groups=mesh['slab'=16,'ang'=2] {'ang'}, dimensions={0}, use_global_device_ids=true | all-gather | bytes 384 | tf_op jit(solution)/shard_map/all_gather | solution.py:104
  324.5 0.2 fusion.17
  324.7 41.4 %all-gather.3.cloned.1.call-done = f32[8,8,4096]{2,1,0:T(8,128)} async-done(((f32[4,8,4096]{2,1,0:T(8,128)}), f32[8,8,4096]{2,1,0:T(8,128)}) %all-gather.3.cloned.1.call-update) | async-done | bytes 1048592 | tf_op jit(solution)/shard_map/all_gather | solution.py:103
  366.1 31.1 %bitcast_add_fusion = f32[8,128,4096]{1,2,0:T(8,128)} fusion(f32[8,128,4096]{1,2,0:T(8,128)} %copy.29, f32[8,128]{1,0:T(8,128)S(1)} %fusion.17, f32[8,8,4096]{2,1,0:T(8,128)} %all-gather.3.cloned.1.call-done, f32[8,256]{1,0:T(8,128)S(1)} %fusion.15, s32[]{:T(128)S(6)} %select_n.12), kind=kOutput, calls=%fused_computation | convolution fusion | flops 411041792 | bytes 34611204 | tf_op jit(solution)/shard_map/ay,azx->zyx/dot_general | solution.py:106
  397.3 17.5 %copy.30 = f32[8,128,4096]{2,1,0:T(8,128)} copy(f32[8,128,4096]{1,2,0:T(8,128)} %bitcast_add_fusion) | data formatting | bytes 33554432
  (11 shorter events, 0.0 us)
Async XLA Ops:
  7.2 0.8 copy-start
  7.2 56.1 %all-reduce.2.cloned.1.call-start = ((), (), s32[]{:S(2)}) async-start(), calls=%async_computation | async-start | bytes 2097152 | tf_op jit(solution)/shard_map/psum | solution.py:85
  8.8 11.6 %copy-start.7 = (s32[1,4]{1,0:T(1,128)S(1)}, s32[1,4]{1,0:T(1,128)}, u32[]{:S(2)}) copy-start(s32[1,4]{1,0:T(1,128)} %param.8) | copy-start | bytes 52
  8.8 11.6 %copy-start.6 = (s32[1,4]{1,0:T(1,128)S(1)}, s32[1,4]{1,0:T(1,128)}, u32[]{:S(2)}) copy-start(s32[1,4]{1,0:T(1,128)} %param.9) | copy-start | bytes 52
  20.4 345.8 %all-gather.3.cloned.1.call-start = ((), (), s32[]{:S(2)}) async-start(), calls=%async_computation.1 | async-start | bytes 1572864 | tf_op jit(solution)/shard_map/all_gather | solution.py:103
  73.1 6.6 %copy-start.2 = (f32[4,160,4096]{2,1,0:T(8,128)}, f32[4,160,4096]{2,1,0:T(8,128)S(1)}, u32[]{:S(2)}) copy-start(f32[4,160,4096]{2,1,0:T(8,128)S(1)} %fusion.7) | copy-start | bytes 31457284
  73.1 158.0 %copy-start.5 = (bf16[4,32,4096]{2,1,0:T(8,128)(2,1)S(1)}, bf16[4,32,4096]{2,1,0:T(8,128)(2,1)}, u32[]{:S(2)}) copy-start(bf16[4,32,4096]{2,1,0:T(8,128)(2,1)} %param.7) | copy-start | bytes 3145732
  79.7 150.1 %collective-permute-start = (f32[4,32,4096]{2,1,0:T(8,128)}, f32[4,32,4096]{2,1,0:T(8,128)S(1)}, u32[]{:S(2)}, u32[]{:S(2)}) collective-permute-start(f32[4,32,4096]{2,1,0:T(8,128)} %get-tuple-element.10), channel_id=1, source_target_pairs={{4,0},{6,2},{8,4},{10,6},{12,8},{14,10},{16,12},{18,14},{20,16},{2... | collective-permute-start | bytes 6291464 | tf_op jit(solution)/shard_map/ppermute | solution.py:13
  81.0 148.8 %collective-permute-start.2 = (f32[4,32,4096]{2,1,0:T(8,128)}, f32[4,32,4096]{2,1,0:T(8,128)}, u32[]{:S(2)}, u32[]{:S(2)}) collective-permute-start(f32[4,32,4096]{2,1,0:T(8,128)} %get-tuple-element.11), channel_id=1, source_target_pairs={{0,2},{2,4},{4,6},{6,8},{8,10},{10,12},{12,14},{14,16},{16,18},{18... | collective-permute-start | bytes 6291464 | tf_op jit(solution)/shard_map/ppermute | solution.py:13
  84.2 145.7 %collective-permute-start.1 = (f32[4,32,4096]{2,1,0:T(8,128)}, f32[4,32,4096]{2,1,0:T(8,128)}, u32[]{:S(2)}, u32[]{:S(2)}) collective-permute-start(f32[4,32,4096]{2,1,0:T(8,128)} %get-tuple-element.12), channel_id=1, source_target_pairs={{2,0},{4,2},{6,4},{8,6},{10,8},{12,10},{14,12},{16,14},{18,16},{20... | collective-permute-start | bytes 6291464 | tf_op jit(solution)/shard_map/ppermute | solution.py:13
  85.4 145.7 %collective-permute-start.3 = (f32[4,32,4096]{2,1,0:T(8,128)}, f32[4,32,4096]{2,1,0:T(8,128)}, u32[]{:S(2)}, u32[]{:S(2)}) collective-permute-start(f32[4,32,4096]{2,1,0:T(8,128)} %get-tuple-element.13), channel_id=1, source_target_pairs={{0,4},{2,6},{4,8},{6,10},{8,12},{10,14},{12,16},{14,18},{16,20},{1... | collective-permute-start | bytes 6291464 | tf_op jit(solution)/shard_map/ppermute | solution.py:13
  92.8 103.9 %collective-permute-start.7 = (f32[4,32]{1,0:T(4,128)S(1)}, f32[4,32]{1,0:T(4,128)S(1)}, u32[]{:S(2)}, u32[]{:S(2)}) collective-permute-start(f32[4,32]{1,0:T(4,128)S(1)} %bitcast.67), channel_id=1, source_target_pairs={{0,4},{2,6},{4,8},{6,10},{8,12},{10,14},{12,16},{14,18},{16,20},{1... | collective-permute-start | bytes 1544 | tf_op jit(solution)/shard_map/ppermute | solution.py:13
  196.7 5.9 %collective-permute-start.4 = (f32[4,32]{1,0:T(4,128)S(1)}, f32[4,32]{1,0:T(4,128)S(1)}, u32[]{:S(2)}, u32[]{:S(2)}) collective-permute-start(f32[4,32]{1,0:T(4,128)S(1)} %bitcast.66), channel_id=1, source_target_pairs={{4,0},{6,2},{8,4},{10,6},{12,8},{14,10},{16,12},{18,14},{20,16},{2... | collective-permute-start | bytes 1544 | tf_op jit(solution)/shard_map/ppermute | solution.py:13
  202.6 24.1 %collective-permute-start.6 = (f32[4,32]{1,0:T(4,128)S(1)}, f32[4,32]{1,0:T(4,128)S(1)}, u32[]{:S(2)}, u32[]{:S(2)}) collective-permute-start(f32[4,32]{1,0:T(4,128)S(1)} %bitcast.65), channel_id=1, source_target_pairs={{0,2},{2,4},{4,6},{6,8},{8,10},{10,12},{12,14},{14,16},{16,18},{18... | collective-permute-start | bytes 1544 | tf_op jit(solution)/shard_map/ppermute | solution.py:13
  226.7 3.0 collective-permute-start.5
  229.8 1.3 copy-start.4
  236.3 56.3 %copy-start.3 = (f32[4,32,4096]{2,1,0:T(8,128)}, f32[4,32,4096]{2,1,0:T(8,128)S(1)}, u32[]{:S(2)}) copy-start(f32[4,32,4096]{2,1,0:T(8,128)S(1)} %fusion.5) | copy-start | bytes 6291460
  236.3 8.5 %collective-permute-start.8 = (f32[4,32,4096]{2,1,0:T(8,128)S(1)}, f32[4,32,4096]{2,1,0:T(8,128)S(1)}, u32[]{:S(2)}, u32[]{:S(2)}) collective-permute-start(f32[4,32,4096]{2,1,0:T(8,128)S(1)} %fusion.5), channel_id=1, source_target_pairs={{0,2},{2,4},{4,6},{6,8},{8,10},{10,12},{12,14},{14,16},{16,18},{18... | collective-permute-start | bytes 6291464 | tf_op jit(solution)/shard_map/ppermute | solution.py:23
  241.2 47.4 %collective-permute-start.10 = (f32[4,32,4096]{2,1,0:T(8,128)S(1)}, f32[4,32,4096]{2,1,0:T(8,128)S(1)}, u32[]{:S(2)}, u32[]{:S(2)}) collective-permute-start(f32[4,32,4096]{2,1,0:T(8,128)S(1)} %fusion.5), channel_id=1, source_target_pairs={{2,0},{4,2},{6,4},{8,6},{10,8},{12,10},{14,12},{16,14},{18,16},{20... | collective-permute-start | bytes 6291464 | tf_op jit(solution)/shard_map/ppermute | solution.py:24
  244.8 47.4 %collective-permute-start.9 = (f32[4,32,4096]{2,1,0:T(8,128)S(1)}, f32[4,32,4096]{2,1,0:T(8,128)S(1)}, u32[]{:S(2)}, u32[]{:S(2)}) collective-permute-start(f32[4,32,4096]{2,1,0:T(8,128)S(1)} %collective-permute-done.8), channel_id=1, source_target_pairs={{0,2},{2,4},{4,6},{6,8},{8,10},{10,12},{12,14},{14,16},{16,18},{18... | collective-permute-start | bytes 6291464 | tf_op jit(solution)/shard_map/ppermute | solution.py:23
  288.6 7.9 %collective-permute-start.11 = (f32[4,32,4096]{2,1,0:T(8,128)S(1)}, f32[4,32,4096]{2,1,0:T(8,128)S(1)}, u32[]{:S(2)}, u32[]{:S(2)}) collective-permute-start(f32[4,32,4096]{2,1,0:T(8,128)S(1)} %collective-permute-done.10), channel_id=1, source_target_pairs={{2,0},{4,2},{6,4},{8,6},{10,8},{12,10},{14,12},{16,14},{18,16},{20... | collective-permute-start | bytes 6291464 | tf_op jit(solution)/shard_map/ppermute | solution.py:24
  397.3 17.5 %copy-start.1 = (f32[64,256]{1,0:T(8,128)S(1)}, f32[64,256]{1,0:T(8,128)}, u32[]{:S(2)}) copy-start(f32[64,256]{1,0:T(8,128)} %param.11) | copy-start | bytes 196612
Sparse Core Ops, SparseCore 0:
  20.5 42.7 all-reduce.1
  302.7 63.4 all-gather.2
where the time goes:
time: 423 us; the launch traced here: 422 us
  waiting for transfers between devices  199 us (47%)
  starting transfers between devices  93.7 us (22%)
  matrix products  58 us (14%)
  local copies, waits for them, and re-layouts  46 us (11%)
  between operations  14.3 us (3%)
  other arithmetic  5.68 us (1%)
  blocking collectives  4.55 us (1%)
    ppermute x8, waiting for transfers between devices, from_behind(): lax.ppermute(value, axis, [(source, source + steps) for source in range(l...  107 us
    ppermute x2, starting transfers between devices, with_halo(): before = lax.ppermute(last, axis, up)  48.6 us
    psum x1, waiting for transfers between devices, body(): summed_all = lax.psum(ray_part, 'ang')  42.6 us
    ppermute x8, starting transfers between devices, from_behind(): lax.ppermute(value, axis, [(source, source + steps) for source in range(l...  42.4 us
    all_gather x1, waiting for transfers between devices, body(): lax.all_gather(back, 'ang', axis=0, tiled=True)  41.4 us
    unnamed x22, local copies, waits for them, and re-layouts  41 us
    dot_general x1, matrix products, body(): update = jnp.einsum('ay,azx->zyx', weights_cells, back_all, precision=high)  31.1 us
    dot_general x1, matrix products, body(): ray_part = jnp.einsum('ay,zyx->azx', weights_cells, volume, precision=high)  11.5 us
  transfers between devices with their start and end apart: 14, of which 9 were waited for; matrix products, arithmetic and copies ran while one was open for 5% of the time, Pallas kernels for 0%

commit v1 on v0

v1 whole, which is shorter than its diff:
```python
import functools

import jax
import jax.numpy as jnp
from jax import lax
from jax.experimental import pallas as pl
from jax.experimental.pallas import tpu as pltpu
from jax.sharding import PartitionSpec as P

F32, BF16 = jnp.float32, jnp.bfloat16
CHUNKS = 2
TILE = 512
LANES = 128
SUBLANES = 8
VMEM = 56 * 1024 * 1024


def split(value):
    high = value.astype(BF16)
    return high, (value - high.astype(F32)).astype(BF16)


def dot(a, b):
    return jnp.dot(a, b, preferred_element_type=F32)


def dot3(a, b):
    ah, al = split(a)
    bh, bl = split(b)
    return dot(ah, bh) + (dot(ah, bl) + dot(al, bh))


def iota(shape, dim):
    return lax.broadcasted_iota(jnp.int32, shape, dim)


def pick(index, values):
    out = jnp.zeros(index.shape, values[0].dtype)
    for at, value in enumerate(values):
        out = jnp.where(index == at, value, out)
    return out


def slice_weights(dims, sign, pos_ref, order_ref, table_ref, rows_ref):
    per, groups, zb, cells = dims
    ang = pos_ref[1]
    for d in range(groups):
        group = lax.rem(ang + sign * d + groups, groups)
        for z in range(zb):
            for a in range(per):
                at = (d * zb + z) * per + a
                rows_ref[at:at + 1, :] = table_ref[pl.ds(order_ref[group * per + a], 1), :]
    wide = rows_ref[...]
    total = wide.shape[1]
    row_slice = lax.rem(iota(wide.shape, 0) // per, zb)
    lane_slice = iota(wide.shape, 1) // cells
    out = jnp.zeros_like(wide)
    for z in range(zb):
        shift = lax.rem(z * cells - ang * cells + total, total)
        here = jnp.logical_and(row_slice == z, lane_slice == z)
        out = jnp.where(here, pltpu.roll(wide, shift, 1), out)
    return out


def rays_kernel(dims, width, tile, extra, pos_ref, order_ref, start_ref, len_ref, table_ref, vol_ref, *refs):
    per, groups, zb, cells = dims
    outs, (rows_ref, left_ref) = refs[:2 * groups], refs[2 * groups:]
    half, t = pl.program_id(0), pl.program_id(1)
    zdev = vol_ref.shape[0]
    count = groups * SUBLANES

    @pl.when(jnp.logical_and(half == 0, t == 0))
    def _():
        weights = slice_weights(dims, 1, pos_ref, order_ref, table_ref, rows_ref)
        high, low = split(weights)
        both = jnp.concatenate([high, low], axis=0)
        left_ref[...] = jnp.concatenate([both, both], axis=1)
        if extra:
            shape = (zdev * per, LANES)
            angle, lane = lax.rem(iota(shape, 0), per), iota(shape, 1)
            starts = pick(angle, [start_ref[0, a].astype(F32) for a in range(per)])
            lengths = pick(angle, [len_ref[0, a].astype(F32) for a in range(per)])
            foot = jnp.where(lane == 0, starts, jnp.where(lane == 1, lengths, 0.0))
            for h in range(2):
                for d in range(groups):
                    outs[h * groups + d][:, width:] = foot if d == 0 else jnp.zeros_like(foot)

    left = left_ref[...]
    columns = pl.ds(pl.multiple_of(t * tile, tile), tile)
    for zp in range(zdev // zb):
        parts = [split(vol_ref[zp * zb + z]) for z in range(zb)]
        right = jnp.concatenate([p[0] for p in parts] + [p[1] for p in parts], axis=0)
        product = dot(left, right)
        sums = product[:count] + product[count:]
        for h in range(2):
            @pl.when(half == h)
            def _():
                for d in range(groups):
                    outs[h * groups + d][zp * SUBLANES:(zp + 1) * SUBLANES, columns] = (
                        sums[d * SUBLANES:(d + 1) * SUBLANES]
                    )


def ray_sums(dims, chunk, pos, order, foot_start, foot_len, table, volume):
    per, groups, zb, cells = dims
    zdev, _, total = volume.shape
    half = total // 2
    width = half // CHUNKS
    tile = min(TILE, width)
    steps = width // tile
    extra = LANES if chunk == 0 else 0
    out = jax.ShapeDtypeStruct((zdev * per, width + extra), F32)
    grid = pltpu.PrefetchScalarGridSpec(
        num_scalar_prefetch=4,
        grid=(2, steps),
        in_specs=[
            pl.BlockSpec(table.shape, lambda h, t, *_: (0, 0)),
            pl.BlockSpec(
                (zdev, cells, tile),
                lambda h, t, pos, *_: (0, 0, lax.rem(pos[0] + h, 2) * (half // tile) + chunk * steps + t),
            ),
        ],
        out_specs=[pl.BlockSpec(out.shape, lambda h, t, *_: (0, 0))] * (2 * groups),
        scratch_shapes=[
            pltpu.VMEM((groups * SUBLANES, table.shape[1]), F32),
            pltpu.VMEM((2 * groups * SUBLANES, 2 * zb * cells), BF16),
        ],
    )
    size = zdev * cells * width * 2
    return pl.pallas_call(
        functools.partial(rays_kernel, dims, width, tile, extra),
        grid_spec=grid,
        out_shape=[out] * (2 * groups),
        compiler_params=pltpu.CompilerParams(vmem_limit_bytes=VMEM),
        cost_estimate=pl.CostEstimate(flops=2 * size * 16, bytes_accessed=size * 4, transcendentals=0),
        name=f"ray_sums_{chunk}",
    )(pos, order, foot_start, foot_len, table, volume)


def residual_kernel(
    dims, rdev, zdev, width, extra, pos_ref, order_ref, table_ref, own_ref, near_ref, far_ref,
    own_foot, near_foot, far_foot, mine_ref, theirs_ref, _, res_ref, sent_ref, own_out, near_out, far_out,
):
    per, groups, zb, cells = dims
    slab, ang = pos_ref[0], pos_ref[1]
    block = zdev * per
    count, rows = 6 * block, 2 * per * rdev
    odd = lax.rem(slab, 2)
    sibling = slab + 1 - 2 * odd
    shape = (count, rows)
    foot = jnp.concatenate(
        [r[i] for r in (own_foot, near_foot, far_foot) for i in range(2)], axis=0
    )
    start, length = foot[:, 0:1], foot[:, 1:2]
    at = iota((count, 1), 0)
    at_in = lax.rem(at, block)
    slice_at = (at_in // (zb * per)) * zb + lax.rem(at_in // per, zb)
    span = jnp.where(length > 0.0, length, 1.0) / zdev
    centre = start + (slice_at.astype(F32) + 0.5) * span
    row_id = iota((1, rows), 1)
    row_slab = jnp.where(row_id // (per * rdev) == 0, slab, sibling)
    row = (row_slab * rdev + lax.rem(row_id, rdev)).astype(F32)
    same_angle = iota(shape, 0) % per == (iota(shape, 1) // rdev) % per
    hat = jnp.maximum(0.0, 1.0 - jnp.abs(row + 0.5 - centre) / span)
    inside = jnp.logical_and(row >= start, row < start + length)
    kernel = jnp.where(jnp.logical_and(same_angle, inside), hat, 0.0)
    if extra:
        weight = jnp.broadcast_to(jnp.sum(kernel, axis=1, keepdims=True), (count, LANES))
        for i, ref in enumerate((own_out, near_out, far_out)):
            for j in range(2):
                ref[j, :, width:] = weight[(2 * i + j) * block:(2 * i + j + 1) * block]
    kernel_t = kernel.T
    cover = jnp.sum(kernel_t, axis=1, keepdims=True)
    angle = lax.rem(iota((rows, 1), 0) // rdev, per)
    path = jnp.zeros((rows, 1), F32)
    for a in range(per):
        total = jnp.sum(table_ref[pl.ds(order_ref[ang * per + a], 1), :], axis=1, keepdims=True)
        path = jnp.where(angle == a, total, path)
    inverse = 1.0 / jnp.maximum(path * cover, 0.25)

    tile = min(TILE, width)
    for t in range(width // tile):
        columns = slice(t * tile, (t + 1) * tile)
        sums = jnp.concatenate(
            [r[i, :, columns] for r in (own_ref, near_ref, far_ref) for i in range(2)], axis=0
        )
        project = dot3(kernel_t, sums)
        measured = jnp.concatenate(
            [
                mine_ref[:, :, columns].astype(F32).reshape(per * rdev, tile),
                theirs_ref[:, :, columns].reshape(per * rdev, tile),
            ],
            axis=0,
        )
        residual = (measured - project) * inverse
        res_ref[:, :, columns] = residual[:per * rdev].reshape(per, rdev, tile)
        sent_ref[:, :, columns] = residual[per * rdev:].reshape(per, rdev, tile)
        back = dot3(kernel, residual)
        for i, ref in enumerate((own_out, near_out, far_out)):
            for j in range(2):
                ref[j, :, columns] = back[(2 * i + j) * block:(2 * i + j + 1) * block]


def residual_step(dims, zdev, chunk, pos, order, table, sums, first, measured, theirs, res):
    per, groups, zb, cells = dims
    _, rdev, total = measured.shape
    half = total // 2
    width = half // CHUNKS
    extra = LANES if chunk == 0 else 0
    block = zdev * per
    full = pl.BlockSpec((2, block, width), lambda i, *_: (0, 0, 0))
    foot = pl.BlockSpec((2, block, LANES), lambda i, *_: (0, 0, width // LANES))
    mine = pl.BlockSpec((per, rdev, width), lambda i, pos, *_: (0, 0, lax.rem(pos[0], 2) * CHUNKS + chunk))
    given = jax.ShapeDtypeStruct((2, block, width + extra), F32)
    whole = pl.BlockSpec(given.shape, lambda i, *_: (0, 0, 0))
    piece = pl.BlockSpec((per, rdev, width), lambda i, *_: (0, 0, 0))
    inputs = [*sums, *first, measured, theirs]
    specs = [full] * 3 + [foot] * 3 + [mine, pl.BlockSpec((per, rdev, width), lambda i, *_: (0, 0, chunk))]
    aliases = {}
    if res is None:
        inputs.append(pos)
        specs.append(pl.BlockSpec(memory_space=pltpu.SMEM))
    else:
        inputs.append(res)
        specs.append(pl.BlockSpec(memory_space=pl.ANY))
        aliases = {2 + 1 + 8: 0}
    flops = 2 * 3 * 2 * 6 * block * 2 * per * rdev * width
    size = 4 * width * (12 * block + 4 * per * rdev)
    return pl.pallas_call(
        functools.partial(residual_kernel, dims, rdev, zdev, width, extra),
        grid_spec=pltpu.PrefetchScalarGridSpec(
            num_scalar_prefetch=2,
            grid=(1,),
            in_specs=[pl.BlockSpec(table.shape, lambda i, *_: (0, 0))] + specs,
            out_specs=[mine, piece, whole, whole, whole],
        ),
        out_shape=[
            jax.ShapeDtypeStruct((per, rdev, total), F32),
            jax.ShapeDtypeStruct((per, rdev, width), F32),
            given, given, given,
        ],
        input_output_aliases=aliases,
        compiler_params=pltpu.CompilerParams(vmem_limit_bytes=VMEM),
        cost_estimate=pl.CostEstimate(flops=flops, bytes_accessed=size, transcendentals=0),
        name=f"residual_{chunk}",
    )(pos, order, table, *inputs)


def update_kernel(dims, width, tile, depth, pos_ref, order_ref, table_ref, vol_ref, *refs):
    per, groups, zb, cells = dims
    backs, refs = refs[:2 * groups], refs[2 * groups:]
    feet, (piece_ref, _, _, out_ref, res_ref, rows_ref, left_ref) = refs[:groups], refs[groups:]
    half, t = pl.program_id(0), pl.program_id(1)
    zdev = vol_ref.shape[0]
    count = groups * SUBLANES

    @pl.when(jnp.logical_and(half == 0, t == 0))
    def _():
        res_ref[...] = piece_ref[...]
        weights = slice_weights(dims, -1, pos_ref, order_ref, table_ref, rows_ref)
        pad = jnp.zeros((depth - 3 * count, weights.shape[1]), F32)
        for zp in range(zdev // zb):
            rows = slice(zp * SUBLANES, (zp + 1) * SUBLANES)
            slices = jnp.concatenate([ref[rows, 0:1] for ref in feet], axis=0)
            scaled = weights / jnp.sum(weights * slices, axis=0, keepdims=True)
            high = scaled.astype(BF16).astype(F32)
            stacked = jnp.concatenate([high, high, scaled - high, pad], axis=0)
            left_ref[zp] = stacked.T.astype(BF16)

    columns = pl.ds(pl.multiple_of(t * tile, tile), tile)
    pad = jnp.zeros((depth - 3 * count, tile), BF16)
    for zp in range(zdev // zb):
        rows = slice(zp * SUBLANES, (zp + 1) * SUBLANES)
        back = jnp.concatenate(
            [jnp.where(half == 0, backs[d][rows, columns], backs[groups + d][rows, columns]) for d in range(groups)],
            axis=0,
        )
        high, low = split(back)
        change = dot(left_ref[zp], jnp.concatenate([high, low, high, pad], axis=0))
        for z in range(zb):
            out_ref[zp * zb + z] = vol_ref[zp * zb + z] + change[z * cells:(z + 1) * cells]


def update_step(dims, chunk, pos, order, table, volume, backs, feet, piece, res, out):
    per, groups, zb, cells = dims
    zdev, _, total = volume.shape
    half = total // 2
    width = half // CHUNKS
    tile = min(TILE, width)
    steps = width // tile
    depth = -(-3 * groups * SUBLANES // LANES) * LANES
    block = zdev * per
    rdev = res.shape[1]
    vol = pl.BlockSpec(
        (zdev, cells, tile),
        lambda h, t, pos, *_: (0, 0, lax.rem(pos[0] + h, 2) * (half // tile) + chunk * steps + t),
    )
    inputs = [table, volume, *backs, *feet, piece, res]
    specs = [pl.BlockSpec(table.shape, lambda h, t, *_: (0, 0)), vol]
    specs += [pl.BlockSpec((block, width), lambda h, t, *_: (0, 0))] * (2 * groups)
    specs += [pl.BlockSpec((block, LANES), lambda h, t, *_: (0, width // LANES))] * groups
    specs += [pl.BlockSpec((per, rdev, width), lambda h, t, *_: (0, 0, 0)), pl.BlockSpec(memory_space=pl.ANY)]
    aliases = {2 + len(inputs) - 1: 1}
    if out is None:
        inputs.append(pos)
        specs.append(pl.BlockSpec(memory_space=pltpu.SMEM))
    else:
        inputs.append(out)
        specs.append(pl.BlockSpec(memory_space=pl.ANY))
        aliases[2 + len(inputs) - 1] = 0
    size = zdev * cells * width * 2
    return pl.pallas_call(
        functools.partial(update_kernel, dims, width, tile, depth),
        grid_spec=pltpu.PrefetchScalarGridSpec(
            num_scalar_prefetch=2,
            grid=(2, steps),
            in_specs=specs,
            out_specs=[
                vol,
                pl.BlockSpec(
                    (per, rdev, width),
                    lambda h, t, pos, *_: (0, 0, (1 - lax.rem(pos[0], 2)) * CHUNKS + chunk),
                ),
            ],
            scratch_shapes=[
                pltpu.VMEM((groups * SUBLANES, table.shape[1]), F32),
                pltpu.VMEM((zdev // zb, zb * cells, depth), BF16),
            ],
        ),
        out_shape=[jax.ShapeDtypeStruct(volume.shape, F32), jax.ShapeDtypeStruct(res.shape, F32)],
        input_output_aliases=aliases,
        compiler_params=pltpu.CompilerParams(vmem_limit_bytes=VMEM),
        cost_estimate=pl.CostEstimate(flops=2 * size * 48, bytes_accessed=size * 8, transcendentals=0),
        name=f"update_{chunk}",
    )(pos, order, *inputs)


def body(volume, measured, foot_start, foot_len, order, table):
    slabs, groups = lax.axis_size("slab"), lax.axis_size("ang")
    per, rdev, total = measured.shape
    zdev, cells, _ = volume.shape
    half = total // 2
    zb = SUBLANES // per
    dims = (per, groups, zb, cells)
    pos = jnp.stack([lax.axis_index("slab"), lax.axis_index("ang")]).astype(jnp.int32)

    def along(value, to):
        pairs = [(s, to(s)) for s in range(slabs) if 0 <= to(s) < slabs]
        return lax.ppermute(value, "slab", pairs)

    def spread(value, other, d):
        if not (other or d):
            return value
        pairs = [
            (s * groups + a, (s ^ other) * groups + (a + d) % groups) for s in range(slabs) for a in range(groups)
        ]
        return lax.ppermute(value, ("slab", "ang"), pairs)

    def facing(s):
        return s ^ 2

    def beyond(s):
        return s - 4 if s & 2 else s + 4

    def back_from_beyond(s):
        return s + 4 if s & 2 else s - 4

    odd = lax.rem(pos[0], 2)
    theirs = along(
        lax.dynamic_slice_in_dim(measured, (1 - odd) * half, half, 2).astype(F32), lambda s: s ^ 1
    )

    sums, res, sent, given = [], None, [], []
    for c in range(CHUNKS):
        parts = ray_sums(dims, c, pos, order, foot_start, foot_len, table, volume)
        parts = [spread(parts[h * groups + d], h, d) for h in range(2) for d in range(groups)]
        own = jnp.stack([sum(parts[:groups]), sum(parts[groups:])])
        near = along(own, facing)
        far = along(near, beyond)
        sums.append((own, near, far))
    for c in range(CHUNKS):
        res, piece, own, near, far = residual_step(
            dims, zdev, c, pos, order, table, sums[c], sums[0], measured, theirs, res
        )
        sent.append(along(piece, lambda s: s ^ 1))
        near = near + along(far, back_from_beyond)
        arrived = along(near, facing)
        halves = [own[i] + arrived[i] for i in range(2)]
        given.append([spread(halves[h], h, d) for h in range(2) for d in range(groups)])
    out = None
    for c in range(CHUNKS):
        out, res = update_step(
            dims, c, pos, order, table, volume, given[c], given[0][:groups], sent[c], res, out
        )
    return out, res


def solution(mesh):
    return jax.shard_map(
        body,
        mesh=mesh,
        in_specs=(
            P("slab", "ang", None),
            P("ang", "slab", None),
            P("slab", "ang"),
            P("slab", "ang"),
            P(),
            P(),
        ),
        out_specs=(P("slab", "ang", None), P("ang", "slab", None)),
        check_vma=False,
    )
```

time: 423 us -> 112 us (0.26)
  waiting for transfers between devices: 199 us -> 34.8 us
  starting transfers between devices: 93.7 us -> 25.1 us
  matrix products: 58 us -> 0 us
  Pallas kernels: 0 us -> 42.2 us
  local copies, waits for them, and re-layouts: 46 us -> 3.91 us
  between operations: 14.3 us -> 0.99 us
  blocking collectives: 4.55 us -> 0 us
    ppermute x12 -> x23, waiting for transfers between devices: 115 us -> 34.8 us  [the longest x11 29 us: along(): return lax.ppermute(value, 'slab', pairs)]
    ppermute x12 -> x23, starting transfers between devices: 93.6 us -> 25.1 us  [the longest x11 15.2 us: along(): return lax.ppermute(value, 'slab', pairs)]
    dot_general x6 -> x0, matrix products: 58 us -> none  [the longest x1 31.1 us: body(): update = jnp.einsum('ay,azx->zyx', weights_cells, back_all, precision=high)]
    psum x1 -> x0, waiting for transfers between devices: 42.6 us -> none  [body(): summed_all = lax.psum(ray_part, 'ang')]
    pallas_call x0 -> x6, Pallas kernels: none -> 42.2 us  [the longest x2 18.1 us: update_step(): pl.pallas_call(functools.partial(update_kernel, dims, width, tile, depth)...]
    all_gather x1 -> x0, waiting for transfers between devices: 41.4 us -> none  [body(): lax.all_gather(back, 'ang', axis=0, tiled=True)]
    unnamed x22 -> x46, local copies, waits for them, and re-layouts: 41 us -> 3.91 us
    div x1 -> x0, other arithmetic: 5.14 us -> none  [body(): res_mine = (measured.astype(jnp.float32) - totals) / denom[:, :, None]]
  transfers between devices with their start and end apart: 14 -> 23, of which waited for: 9 -> 7; matrix products, arithmetic and copies ran while one was open for 5% -> 4% of each run, Pallas kernels for 0% -> 23%
where the time goes in v1:
time: 112 us
  Pallas kernels  42.2 us (38%)
  waiting for transfers between devices  34.8 us (31%)
  starting transfers between devices  25.1 us (22%)
  other arithmetic  4.75 us (4%)
  local copies, waits for them, and re-layouts  3.91 us (3%)
    ppermute x11, waiting for transfers between devices, along(): return lax.ppermute(value, 'slab', pairs)  29 us
    pallas_call x2, Pallas kernels, update_step(): pl.pallas_call(functools.partial(update_kernel, dims, width, tile, depth)...  18.1 us
    ppermute x11, starting transfers between devices, along(): return lax.ppermute(value, 'slab', pairs)  15.2 us
    pallas_call x2, Pallas kernels, ray_sums(): pl.pallas_call(functools.partial(rays_kernel, dims, width, tile, extra),...  14.9 us
    ppermute x12, starting transfers between devices, spread(): return lax.ppermute(value, ('slab', 'ang'), pairs)  9.89 us
    pallas_call x2, Pallas kernels, residual_step(): pl.pallas_call(functools.partial(residual_kernel, dims, rdev, zdev, width...  9.22 us
    ppermute x12, waiting for transfers between devices, spread(): return lax.ppermute(value, ('slab', 'ang'), pairs)  5.8 us
    unnamed x46, local copies, waits for them, and re-layouts  3.91 us
  transfers between devices with their start and end apart: 23, of which 7 were waited for; matrix products, arithmetic and copies ran while one was open for 4% of the time, Pallas kernels for 23%

profile of v1, /device:TPU:0, one launch (start us, length us, event | category | flops | bytes accessed | tf_op | source)
XLA Modules:
  0.0 111.7 jit_solution(14238852304900155000)
XLA Ops:
  0.6 0.6 pad_add_fusion.pos_ref._.refs_8_
  1.3 7.4 %ray_sums_1.1 = (f32[32,1024]{1,0:T(8,128)}, f32[32,1024]{1,0:T(8,128)}, f32[32,1024]{1,0:T(8,128)}, f32[32,1024]{1,0:T(8,128)}) custom-call(s32[2]{0:T(128)} %pad_add_fusion.pos_ref._.refs_8_, s32[64]{0:T(128)} %order_ref.11, s32[1,4]{1,0:T(1,128)} %start_ref.3, s32[1,4]{1,0:T(1,128)} %len_ref.3, f32[64,256]{1,0:T(8,128)} %table_ref.11, f32[8,128,4096]{2,1,0:T(8,128)} %vol_ref.7), custom_call_target="tpu_custom_call" | custom-call | flops 67108864 | bytes 8388608 | tf_op jit(solution)/shard_map/ray_sums_1/pallas_call | solution.py:130
  8.7 3.0 %collective-permute-start = (f32[32,1024]{1,0:T(8,128)}, f32[32,1024]{1,0:T(8,128)S(1)}, u32[]{:S(2)}, u32[]{:S(2)}) collective-permute-start(f32[32,1024]{1,0:T(8,128)} %get-tuple-element.23), channel_id=1, source_target_pairs={{0,1},{1,0},{2,3},{3,2},{4,5},{5,4},{6,7},{7,6},{8,9},{9,8},{10,11... | collective-permute-start | bytes 393224 | tf_op jit(solution)/shard_map/ppermute | solution.py:357
  11.7 7.4 %ray_sums_0.1 = (f32[32,1152]{1,0:T(8,128)}, f32[32,1152]{1,0:T(8,128)}, f32[32,1152]{1,0:T(8,128)}, f32[32,1152]{1,0:T(8,128)}) custom-call(s32[2]{0:T(128)} %pad_add_fusion.pos_ref._.refs_8_, s32[64]{0:T(128)} %order_ref.11, s32[1,4]{1,0:T(1,128)} %start_ref.3, s32[1,4]{1,0:T(1,128)} %len_ref.3, f32[64,256]{1,0:T(8,128)} %table_ref.11, f32[8,128,4096]{2,1,0:T(8,128)} %vol_ref.7), custom_call_target="tpu_custom_call" | custom-call | flops 67108864 | bytes 8388608 | tf_op jit(solution)/shard_map/ray_sums_0/pallas_call | solution.py:130
  19.1 0.2 collective-permute-start.5
  19.3 0.0 collective-permute-start.6
  19.3 2.0 %collective-permute-start.7 = (f32[32,1152]{1,0:T(8,128)}, f32[32,1152]{1,0:T(8,128)S(1)}, u32[]{:S(2)}, u32[]{:S(2)}) collective-permute-start(f32[32,1152]{1,0:T(8,128)} %get-tuple-element.29), channel_id=1, source_target_pairs={{0,3},{1,2},{2,1},{3,0},{4,7},{5,6},{6,5},{7,4},{8,11},{9,10},{10,... | collective-permute-start | bytes 442376 | tf_op jit(solution)/shard_map/ppermute | solution.py:357
  21.3 0.1 dynamic-slice_convert_fusion
  21.4 0.1 collective-permute-start.10
  21.5 4.7 %collective-permute-done.5 = f32[32,1152]{1,0:T(8,128)S(1)} collective-permute-done((f32[32,1152]{1,0:T(8,128)}, f32[32,1152]{1,0:T(8,128)S(1)}, u32[]{:S(2)}, u32[]{:S(2)}) %collective-permute-start.5) | collective-permute-done | bytes 147488 | tf_op jit(solution)/shard_map/ppermute | solution.py:357
  26.2 0.9 add_bitcast_fusion.1
  27.1 0.0 collective-permute-done.6
  27.1 0.0 collective-permute-done.7
  27.2 1.6 %collective-permute-start.8 = (f32[2,32,1152]{2,1,0:T(8,128)S(1)}, f32[2,32,1152]{2,1,0:T(8,128)S(1)}, u32[]{:S(2)}, u32[]{:S(2)}) collective-permute-start(f32[2,32,1152]{2,1,0:T(8,128)S(1)} %pad_maximum_fusion.own_ref.own_foot), channel_id=1, source_target_pairs={{0,4},{2,6},{4,0},{6,2},{8,12},{10,14},{12,8},{14,10},{16,20},{18,... | collective-permute-start | bytes 884744 | tf_op jit(solution)/shard_map/ppermute | solution.py:349
  28.8 0.3 collective-permute-start.1
  29.0 0.3 collective-permute-start.2
  29.4 0.0 collective-permute-done
  29.4 7.4 %collective-permute-done.8.near_ref.near_foot = f32[2,32,1152]{2,1,0:T(8,128)S(1)} collective-permute-done((f32[2,32,1152]{2,1,0:T(8,128)S(1)}, f32[2,32,1152]{2,1,0:T(8,128)S(1)}, u32[]{:S(2)}, u32[]{:S(2)}) %collective-permute-start.8) | collective-permute-done | bytes 294944 | tf_op jit(solution)/shard_map/ppermute | solution.py:349
  36.7 3.5 %collective-permute-start.9 = (f32[2,32,1152]{2,1,0:T(8,128)S(1)}, f32[2,32,1152]{2,1,0:T(8,128)S(1)}, u32[]{:S(2)}, u32[]{:S(2)}) collective-permute-start(f32[2,32,1152]{2,1,0:T(8,128)S(1)} %collective-permute-done.8.near_ref.near_foot), channel_id=1, source_target_pairs={{0,8},{2,10},{8,16},{10,18},{12,4},{14,6},{16,24},{18,26},{20,12},... | collective-permute-start | bytes 884744 | tf_op jit(solution)/shard_map/ppermute | solution.py:349
  40.2 0.0 collective-permute-done.1
  40.2 0.0 collective-permute-done.2
  40.3 0.1 collective-permute-start.3
  40.4 6.0 %collective-permute-done.9.far_ref.far_foot = f32[2,32,1152]{2,1,0:T(8,128)S(1)} collective-permute-done((f32[2,32,1152]{2,1,0:T(8,128)S(1)}, f32[2,32,1152]{2,1,0:T(8,128)S(1)}, u32[]{:S(2)}, u32[]{:S(2)}) %collective-permute-start.9) | collective-permute-done | bytes 294944 | tf_op jit(solution)/shard_map/ppermute | solution.py:349
  46.4 0.0 collective-permute-done.10.theirs_ref
  46.4 0.7 copy-done.4
  47.1 1.0 copy-done.2
  48.1 4.6 %residual_0.1 = (f32[4,32,4096]{2,1,0:T(8,128)}, f32[4,32,1024]{2,1,0:T(8,128)}, f32[2,32,1152]{2,1,0:T(8,128)}, f32[2,32,1152]{2,1,0:T(8,128)}, f32[2,32,1152]{2,1,0:T(8,128)}) custom-call(s32[2]{0:T(128)} %pad_add_fusion.pos_ref._.refs_8_, s32[64]{0:T(128)} %order_ref.11, f32[64,256]{1,0:T(8,128)} %table_ref.11, f32[2,32,1152]{2,1,0:T(8,128)} %copy-done.1, ...), custom_call_target="tpu_custom_call" | custom-call | flops 603979776 | bytes 3670016 | tf_op jit(solution)/shard_map/residual_0/pallas_call | solution.py:229
  52.7 1.3 %collective-permute-start.16 = (f32[2,32,1152]{2,1,0:T(8,128)}, f32[2,32,1152]{2,1,0:T(8,128)S(1)}, u32[]{:S(2)}, u32[]{:S(2)}) collective-permute-start(f32[2,32,1152]{2,1,0:T(8,128)} %get-tuple-element.36), channel_id=1, source_target_pairs={{4,12},{6,14},{8,0},{10,2},{12,20},{14,22},{16,8},{18,10},{20,28},... | collective-permute-start | bytes 884744 | tf_op jit(solution)/shard_map/ppermute | solution.py:349
  54.0 0.0 collective-permute-done.3.near_ref
  54.0 5.0 %collective-permute-start.4 = (f32[2,32,1024]{2,1,0:T(8,128)S(1)}, f32[2,32,1024]{2,1,0:T(8,128)S(1)}, u32[]{:S(2)}, u32[]{:S(2)}) collective-permute-start(f32[2,32,1024]{2,1,0:T(8,128)S(1)} %collective-permute-done.3.near_ref), channel_id=1, source_target_pairs={{0,8},{2,10},{8,16},{10,18},{12,4},{14,6},{16,24},{18,26},{20,12},... | collective-permute-start | bytes 786440 | tf_op jit(solution)/shard_map/ppermute | solution.py:349
  59.0 4.3 %collective-permute-done.16 = f32[2,32,1152]{2,1,0:T(8,128)S(1)} collective-permute-done((f32[2,32,1152]{2,1,0:T(8,128)}, f32[2,32,1152]{2,1,0:T(8,128)S(1)}, u32[]{:S(2)}, u32[]{:S(2)}) %collective-permute-start.16) | collective-permute-done | bytes 294944 | tf_op jit(solution)/shard_map/ppermute | solution.py:349
  63.3 1.0 add.53
  64.3 0.9 collective-permute-start.17
  65.3 0.0 collective-permute-done.4.far_ref
  65.3 0.7 copy-done.13
  66.0 4.6 %residual_1.1 = (f32[4,32,4096]{2,1,0:T(8,128)}, f32[4,32,1024]{2,1,0:T(8,128)}, f32[2,32,1024]{2,1,0:T(8,128)}, f32[2,32,1024]{2,1,0:T(8,128)}, f32[2,32,1024]{2,1,0:T(8,128)}) custom-call(s32[2]{0:T(128)} %pad_add_fusion.pos_ref._.refs_8_, s32[64]{0:T(128)} %order_ref.11, f32[64,256]{1,0:T(8,128)} %table_ref.11, ...), custom_call_target="tpu_custom_call", output_to_operand_aliasing={{0}: (11, {})} | custom-call | flops 603979776 | bytes 3670016 | tf_op jit(solution)/shard_map/residual_1/pallas_call | solution.py:229
  70.6 1.3 %collective-permute-start.11 = (f32[2,32,1024]{2,1,0:T(8,128)}, f32[2,32,1024]{2,1,0:T(8,128)S(1)}, u32[]{:S(2)}, u32[]{:S(2)}) collective-permute-start(f32[2,32,1024]{2,1,0:T(8,128)} %get-tuple-element.33), channel_id=1, source_target_pairs={{4,12},{6,14},{8,0},{10,2},{12,20},{14,22},{16,8},{18,10},{20,28},... | collective-permute-start | bytes 786440 | tf_op jit(solution)/shard_map/ppermute | solution.py:349
  71.9 0.1 collective-permute-start.19
  72.0 0.5 collective-permute-start.22
  72.5 7.0 %collective-permute-done.11 = f32[2,32,1024]{2,1,0:T(8,128)S(1)} collective-permute-done((f32[2,32,1024]{2,1,0:T(8,128)}, f32[2,32,1024]{2,1,0:T(8,128)S(1)}, u32[]{:S(2)}, u32[]{:S(2)}) %collective-permute-start.11) | collective-permute-done | bytes 262176 | tf_op jit(solution)/shard_map/ppermute | solution.py:349
  79.4 1.0 add.48
  80.4 1.0 collective-permute-start.12
  81.4 0.0 collective-permute-done.17
  81.4 0.1 collective-permute-start.21
  81.5 1.0 collective-permute-start.20
  82.5 4.4 %collective-permute-done.12 = f32[2,32,1024]{2,1,0:T(8,128)S(1)} collective-permute-done((f32[2,32,1024]{2,1,0:T(8,128)S(1)}, f32[2,32,1024]{2,1,0:T(8,128)S(1)}, u32[]{:S(2)}, u32[]{:S(2)}) %collective-permute-start.12) | collective-permute-done | bytes 262176 | tf_op jit(solution)/shard_map/ppermute | solution.py:349
  86.8 0.9 collective-permute-start.18
  87.7 1.0 fusion.2
  88.7 0.0 collective-permute-done.22.refs_6_
  88.8 0.1 collective-permute-start.15
  88.8 0.0 collective-permute-done.21.refs_3_
  88.9 1.2 %collective-permute-start.14 = (f32[32,1024]{1,0:T(8,128)S(1)}, f32[32,1024]{1,0:T(8,128)S(1)}, u32[]{:S(2)}, u32[]{:S(2)}) collective-permute-start(f32[32,1024]{1,0:T(8,128)S(1)} %get-tuple-element.44), channel_id=1, source_target_pairs={{0,2},{1,3},{2,0},{3,1},{4,6},{5,7},{6,4},{7,5},{8,10},{9,11},{10,... | collective-permute-start | bytes 393224 | tf_op jit(solution)/shard_map/ppermute | solution.py:357
  90.1 0.0 collective-permute-done.20.refs_2_
  90.1 0.9 collective-permute-start.13
  91.0 1.1 collective-permute-done.18.refs_1_.refs_5_
  92.1 0.6 copy-done.6
  92.8 9.1 %update_0.1 = (f32[8,128,4096]{2,1,0:T(8,128)}, f32[4,32,4096]{2,1,0:T(8,128)}) custom-call(s32[2]{0:T(128)} %pad_add_fusion.pos_ref._.refs_8_, s32[64]{0:T(128)} %order_ref.11, f32[64,256]{1,0:T(8,128)} %table_ref.11, f32[8,128,4096]{2,1,0:T(8,128)} %vol_ref.7, f32[32,1152]{1,0:T(8,128)} %copy-done.5, ...), custom_call_target="tpu_custom_call", output_to_operand_aliasing={{1}: (11, {})} | custom-call | flops 201326592 | bytes 16777216 | tf_op jit(solution)/shard_map/update_0/pallas_call | solution.py:312
  101.8 0.0 collective-permute-done.19.refs_6_
  101.8 0.0 collective-permute-done.15.refs_3_
  101.9 0.7 copy-done.8
  102.6 0.0 copy-done.16
  102.6 0.0 copy-done.17
  102.7 0.0 copy-done.18
  102.7 9.0 %update_1.1 = (f32[8,128,4096]{2,1,0:T(8,128)}, f32[4,32,4096]{2,1,0:T(8,128)}) custom-call(s32[2]{0:T(128)} %pad_add_fusion.pos_ref._.refs_8_, s32[64]{0:T(128)} %order_ref.11, f32[64,256]{1,0:T(8,128)} %table_ref.11, f32[8,128,4096]{2,1,0:T(8,128)} %vol_ref.7, f32[32,1024]{1,0:T(8,128)} %copy-done.9, ...), custom_call_target="tpu_custom_call", output_to_operand_aliasing={{1}: (11, {}), {0}: (12, {})} | custom-call | flops 201326592 | bytes 16777216 | tf_op jit(solution)/shard_map/update_1/pallas_call | solution.py:312
  (46 shorter events, 0.2 us)
Async XLA Ops:
  8.7 12.6 %copy-start = (bf16[4,32,4096]{2,1,0:T(8,128)(2,1)S(1)}, bf16[4,32,4096]{2,1,0:T(8,128)(2,1)}, u32[]{:S(2)}) copy-start(bf16[4,32,4096]{2,1,0:T(8,128)(2,1)} %mine_ref.3) | copy-start | bytes 3145732
  8.7 20.6 %collective-permute-start = (f32[32,1024]{1,0:T(8,128)}, f32[32,1024]{1,0:T(8,128)S(1)}, u32[]{:S(2)}, u32[]{:S(2)}) collective-permute-start(f32[32,1024]{1,0:T(8,128)} %get-tuple-element.23), channel_id=1, source_target_pairs={{0,1},{1,0},{2,3},{3,2},{4,5},{5,4},{6,7},{7,6},{8,9},{9,8},{10,11... | collective-permute-start | bytes 393224 | tf_op jit(solution)/shard_map/ppermute | solution.py:357
  19.1 9.6 %copy-start.22 = (f32[32,1024]{1,0:T(8,128)S(1)}, f32[32,1024]{1,0:T(8,128)}, u32[]{:S(2)}) copy-start(f32[32,1024]{1,0:T(8,128)} %get-tuple-element.24) | copy-start | bytes 393220
  19.1 9.9 %copy-start.21 = (f32[32,1024]{1,0:T(8,128)S(1)}, f32[32,1024]{1,0:T(8,128)}, u32[]{:S(2)}) copy-start(f32[32,1024]{1,0:T(8,128)} %get-tuple-element.25) | copy-start | bytes 393220
  19.1 10.2 %copy-start.19 = (f32[32,1024]{1,0:T(8,128)S(1)}, f32[32,1024]{1,0:T(8,128)}, u32[]{:S(2)}) copy-start(f32[32,1024]{1,0:T(8,128)} %get-tuple-element.22) | copy-start | bytes 393220
  19.1 7.0 %collective-permute-start.5 = (f32[32,1152]{1,0:T(8,128)}, f32[32,1152]{1,0:T(8,128)S(1)}, u32[]{:S(2)}, u32[]{:S(2)}) collective-permute-start(f32[32,1152]{1,0:T(8,128)} %get-tuple-element.27), channel_id=1, source_target_pairs={{0,1},{1,0},{2,3},{3,2},{4,5},{5,4},{6,7},{7,6},{8,9},{9,8},{10,11... | collective-permute-start | bytes 442376 | tf_op jit(solution)/shard_map/ppermute | solution.py:357
  19.3 7.8 %collective-permute-start.6 = (f32[32,1152]{1,0:T(8,128)}, f32[32,1152]{1,0:T(8,128)S(1)}, u32[]{:S(2)}, u32[]{:S(2)}) collective-permute-start(f32[32,1152]{1,0:T(8,128)} %get-tuple-element.28), channel_id=1, source_target_pairs={{0,2},{1,3},{2,0},{3,1},{4,6},{5,7},{6,4},{7,5},{8,10},{9,11},{10,... | collective-permute-start | bytes 442376 | tf_op jit(solution)/shard_map/ppermute | solution.py:357
  19.3 7.8 %collective-permute-start.7 = (f32[32,1152]{1,0:T(8,128)}, f32[32,1152]{1,0:T(8,128)S(1)}, u32[]{:S(2)}, u32[]{:S(2)}) collective-permute-start(f32[32,1152]{1,0:T(8,128)} %get-tuple-element.29), channel_id=1, source_target_pairs={{0,3},{1,2},{2,1},{3,0},{4,7},{5,6},{6,5},{7,4},{8,11},{9,10},{10,... | collective-permute-start | bytes 442376 | tf_op jit(solution)/shard_map/ppermute | solution.py:357
  21.4 25.0 %collective-permute-start.10 = (f32[4,32,2048]{2,1,0:T(8,128)S(1)}, f32[4,32,2048]{2,1,0:T(8,128)S(1)}, u32[]{:S(2)}, u32[]{:S(2)}) collective-permute-start(f32[4,32,2048]{2,1,0:T(8,128)S(1)} %dynamic-slice_convert_fusion), channel_id=1, source_target_pairs={{0,2},{2,0},{4,6},{6,4},{8,10},{10,8},{12,14},{14,12},{16,18},{18,... | collective-permute-start | bytes 3145736 | tf_op jit(solution)/shard_map/ppermute | solution.py:349
  27.2 19.2 %copy-start.1 = (f32[2,32,1152]{2,1,0:T(8,128)}, f32[2,32,1152]{2,1,0:T(8,128)S(1)}, u32[]{:S(2)}) copy-start(f32[2,32,1152]{2,1,0:T(8,128)S(1)} %pad_maximum_fusion.own_ref.own_foot) | copy-start | bytes 884740
  27.2 9.5 %collective-permute-start.8 = (f32[2,32,1152]{2,1,0:T(8,128)S(1)}, f32[2,32,1152]{2,1,0:T(8,128)S(1)}, u32[]{:S(2)}, u32[]{:S(2)}) collective-permute-start(f32[2,32,1152]{2,1,0:T(8,128)S(1)} %pad_maximum_fusion.own_ref.own_foot), channel_id=1, source_target_pairs={{0,4},{2,6},{4,0},{6,2},{8,12},{10,14},{12,8},{14,10},{16,20},{18,... | collective-permute-start | bytes 884744 | tf_op jit(solution)/shard_map/ppermute | solution.py:349
  28.8 11.5 %collective-permute-start.1 = (f32[32,1024]{1,0:T(8,128)S(1)}, f32[32,1024]{1,0:T(8,128)S(1)}, u32[]{:S(2)}, u32[]{:S(2)}) collective-permute-start(f32[32,1024]{1,0:T(8,128)S(1)} %copy-done.22), channel_id=1, source_target_pairs={{0,2},{1,3},{2,0},{3,1},{4,6},{5,7},{6,4},{7,5},{8,10},{9,11},{10,... | collective-permute-start | bytes 393224 | tf_op jit(solution)/shard_map/ppermute | solution.py:357
  29.0 11.2 %collective-permute-start.2 = (f32[32,1024]{1,0:T(8,128)S(1)}, f32[32,1024]{1,0:T(8,128)S(1)}, u32[]{:S(2)}, u32[]{:S(2)}) collective-permute-start(f32[32,1024]{1,0:T(8,128)S(1)} %copy-done.21), channel_id=1, source_target_pairs={{0,3},{1,2},{2,1},{3,0},{4,7},{5,6},{6,5},{7,4},{8,11},{9,10},{10,... | collective-permute-start | bytes 393224 | tf_op jit(solution)/shard_map/ppermute | solution.py:357
  36.7 9.7 %copy-start.3 = (f32[2,32,1152]{2,1,0:T(8,128)}, f32[2,32,1152]{2,1,0:T(8,128)S(1)}, u32[]{:S(2)}) copy-start(f32[2,32,1152]{2,1,0:T(8,128)S(1)} %collective-permute-done.8.near_ref.near_foot) | copy-start | bytes 884740
  36.7 9.7 %collective-permute-start.9 = (f32[2,32,1152]{2,1,0:T(8,128)S(1)}, f32[2,32,1152]{2,1,0:T(8,128)S(1)}, u32[]{:S(2)}, u32[]{:S(2)}) collective-permute-start(f32[2,32,1152]{2,1,0:T(8,128)S(1)} %collective-permute-done.8.near_ref.near_foot), channel_id=1, source_target_pairs={{0,8},{2,10},{8,16},{10,18},{12,4},{14,6},{16,24},{18,26},{20,12},... | collective-permute-start | bytes 884744 | tf_op jit(solution)/shard_map/ppermute | solution.py:349
  40.3 25.0 %copy-start.7 = (f32[2,32,1024]{2,1,0:T(8,128)}, f32[2,32,1024]{2,1,0:T(8,128)S(1)}, u32[]{:S(2)}) copy-start(f32[2,32,1024]{2,1,0:T(8,128)S(1)} %pad_maximum_fusion.1.own_ref) | copy-start | bytes 786436
  40.3 13.7 %collective-permute-start.3 = (f32[2,32,1024]{2,1,0:T(8,128)S(1)}, f32[2,32,1024]{2,1,0:T(8,128)S(1)}, u32[]{:S(2)}, u32[]{:S(2)}) collective-permute-start(f32[2,32,1024]{2,1,0:T(8,128)S(1)} %pad_maximum_fusion.1.own_ref), channel_id=1, source_target_pairs={{0,4},{2,6},{4,0},{6,2},{8,12},{10,14},{12,8},{14,10},{16,20},{18,... | collective-permute-start | bytes 786440 | tf_op jit(solution)/shard_map/ppermute | solution.py:349
  46.4 0.7 copy-start.4
  47.1 1.0 copy-start.2
  52.7 10.7 %collective-permute-start.16 = (f32[2,32,1152]{2,1,0:T(8,128)}, f32[2,32,1152]{2,1,0:T(8,128)S(1)}, u32[]{:S(2)}, u32[]{:S(2)}) collective-permute-start(f32[2,32,1152]{2,1,0:T(8,128)} %get-tuple-element.36), channel_id=1, source_target_pairs={{4,12},{6,14},{8,0},{10,2},{12,20},{14,22},{16,8},{18,10},{20,28},... | collective-permute-start | bytes 884744 | tf_op jit(solution)/shard_map/ppermute | solution.py:349
  54.0 11.3 %copy-start.12 = (f32[2,32,1024]{2,1,0:T(8,128)}, f32[2,32,1024]{2,1,0:T(8,128)S(1)}, u32[]{:S(2)}) copy-start(f32[2,32,1024]{2,1,0:T(8,128)S(1)} %collective-permute-done.3.near_ref) | copy-start | bytes 786436
  54.0 11.3 %collective-permute-start.4 = (f32[2,32,1024]{2,1,0:T(8,128)S(1)}, f32[2,32,1024]{2,1,0:T(8,128)S(1)}, u32[]{:S(2)}, u32[]{:S(2)}) collective-permute-start(f32[2,32,1024]{2,1,0:T(8,128)S(1)} %collective-permute-done.3.near_ref), channel_id=1, source_target_pairs={{0,8},{2,10},{8,16},{10,18},{12,4},{14,6},{16,24},{18,26},{20,12},... | collective-permute-start | bytes 786440 | tf_op jit(solution)/shard_map/ppermute | solution.py:349
  64.3 17.0 %collective-permute-start.17 = (f32[2,32,1152]{2,1,0:T(8,128)S(1)}, f32[2,32,1152]{2,1,0:T(8,128)S(1)}, u32[]{:S(2)}, u32[]{:S(2)}) collective-permute-start(f32[2,32,1152]{2,1,0:T(8,128)S(1)} %add.53), channel_id=1, source_target_pairs={{0,4},{2,6},{4,0},{6,2},{8,12},{10,14},{12,8},{14,10},{16,20},{18,... | collective-permute-start | bytes 884744 | tf_op jit(solution)/shard_map/ppermute | solution.py:349
  65.3 0.7 copy-start.13
  66.0 6.0 %copy-start.20 = (f32[4,32,1024]{2,1,0:T(8,128)S(1)}, f32[4,32,1024]{2,1,0:T(8,128)}, u32[]{:S(2)}) copy-start(f32[4,32,1024]{2,1,0:T(8,128)} %get-tuple-element.38) | copy-start | bytes 1572868
  66.0 15.4 %copy-start.11 = (f32[2,32,1152]{2,1,0:T(8,128)S(1)}, f32[2,32,1152]{2,1,0:T(8,128)}, u32[]{:S(2)}) copy-start(f32[2,32,1152]{2,1,0:T(8,128)} %get-tuple-element.34) | copy-start | bytes 884740
  70.6 8.8 %collective-permute-start.11 = (f32[2,32,1024]{2,1,0:T(8,128)}, f32[2,32,1024]{2,1,0:T(8,128)S(1)}, u32[]{:S(2)}, u32[]{:S(2)}) collective-permute-start(f32[2,32,1024]{2,1,0:T(8,128)} %get-tuple-element.33), channel_id=1, source_target_pairs={{4,12},{6,14},{8,0},{10,2},{12,20},{14,22},{16,8},{18,10},{20,28},... | collective-permute-start | bytes 786440 | tf_op jit(solution)/shard_map/ppermute | solution.py:349
  71.9 29.9 %collective-permute-start.19 = (f32[4,32,1024]{2,1,0:T(8,128)}, f32[4,32,1024]{2,1,0:T(8,128)S(1)}, u32[]{:S(2)}, u32[]{:S(2)}) collective-permute-start(f32[4,32,1024]{2,1,0:T(8,128)} %get-tuple-element.37), channel_id=1, source_target_pairs={{0,2},{2,0},{4,6},{6,4},{8,10},{10,8},{12,14},{14,12},{16,18},{18,... | collective-permute-start | bytes 1572872 | tf_op jit(solution)/shard_map/ppermute | solution.py:349
  72.0 16.8 %collective-permute-start.22 = (f32[4,32,1024]{2,1,0:T(8,128)S(1)}, f32[4,32,1024]{2,1,0:T(8,128)S(1)}, u32[]{:S(2)}, u32[]{:S(2)}) collective-permute-start(f32[4,32,1024]{2,1,0:T(8,128)S(1)} %copy-done.20), channel_id=1, source_target_pairs={{0,2},{2,0},{4,6},{6,4},{8,10},{10,8},{12,14},{14,12},{16,18},{18,... | collective-permute-start | bytes 1572872 | tf_op jit(solution)/shard_map/ppermute | solution.py:349
  80.4 6.4 %collective-permute-start.12 = (f32[2,32,1024]{2,1,0:T(8,128)S(1)}, f32[2,32,1024]{2,1,0:T(8,128)S(1)}, u32[]{:S(2)}, u32[]{:S(2)}) collective-permute-start(f32[2,32,1024]{2,1,0:T(8,128)S(1)} %add.48), channel_id=1, source_target_pairs={{0,4},{2,6},{4,0},{6,2},{8,12},{10,14},{12,8},{14,10},{16,20},{18,... | collective-permute-start | bytes 786440 | tf_op jit(solution)/shard_map/ppermute | solution.py:349
  81.4 10.7 %copy-start.5 = (f32[32,1152]{1,0:T(8,128)}, f32[32,1152]{1,0:T(8,128)S(1)}, u32[]{:S(2)}) copy-start(f32[32,1152]{1,0:T(8,128)S(1)} %get-tuple-element.43.refs_0_.refs_4_) | copy-start | bytes 442372
  81.4 7.4 %collective-permute-start.21 = (f32[32,1152]{1,0:T(8,128)S(1)}, f32[32,1152]{1,0:T(8,128)S(1)}, u32[]{:S(2)}, u32[]{:S(2)}) collective-permute-start(f32[32,1152]{1,0:T(8,128)S(1)} %get-tuple-element.42), channel_id=1, source_target_pairs={{0,3},{1,2},{2,1},{3,0},{4,7},{5,6},{6,5},{7,4},{8,11},{9,10},{10,... | collective-permute-start | bytes 442376 | tf_op jit(solution)/shard_map/ppermute | solution.py:357
  81.5 8.6 %collective-permute-start.20 = (f32[32,1152]{1,0:T(8,128)S(1)}, f32[32,1152]{1,0:T(8,128)S(1)}, u32[]{:S(2)}, u32[]{:S(2)}) collective-permute-start(f32[32,1152]{1,0:T(8,128)S(1)} %get-tuple-element.42), channel_id=1, source_target_pairs={{0,2},{1,3},{2,0},{3,1},{4,6},{5,7},{6,4},{7,5},{8,10},{9,11},{10,... | collective-permute-start | bytes 442376 | tf_op jit(solution)/shard_map/ppermute | solution.py:357
  86.8 5.3 %collective-permute-start.18 = (f32[32,1152]{1,0:T(8,128)S(1)}, f32[32,1152]{1,0:T(8,128)S(1)}, u32[]{:S(2)}, u32[]{:S(2)}) collective-permute-start(f32[32,1152]{1,0:T(8,128)S(1)} %get-tuple-element.43.refs_0_.refs_4_), channel_id=1, source_target_pairs={{0,1},{1,0},{2,3},{3,2},{4,5},{5,4},{6,7},{7,6},{8,9},{9,8},{10,11... | collective-permute-start | bytes 442376 | tf_op jit(solution)/shard_map/ppermute | solution.py:357
  88.7 13.1 %copy-start.9 = (f32[32,1024]{1,0:T(8,128)}, f32[32,1024]{1,0:T(8,128)S(1)}, u32[]{:S(2)}) copy-start(f32[32,1024]{1,0:T(8,128)S(1)} %get-tuple-element.45.refs_0_) | copy-start | bytes 393220
  88.8 3.4 %copy-start.10 = (f32[4,32,1024]{2,1,0:T(8,128)}, f32[4,32,1024]{2,1,0:T(8,128)S(1)}, u32[]{:S(2)}) copy-start(f32[4,32,1024]{2,1,0:T(8,128)S(1)} %collective-permute-done.22.refs_6_) | copy-start | bytes 1572868
  88.8 13.1 %collective-permute-start.15 = (f32[32,1024]{1,0:T(8,128)S(1)}, f32[32,1024]{1,0:T(8,128)S(1)}, u32[]{:S(2)}, u32[]{:S(2)}) collective-permute-start(f32[32,1024]{1,0:T(8,128)S(1)} %get-tuple-element.44), channel_id=1, source_target_pairs={{0,3},{1,2},{2,1},{3,0},{4,7},{5,6},{6,5},{7,4},{8,11},{9,10},{10,... | collective-permute-start | bytes 393224 | tf_op jit(solution)/shard_map/ppermute | solution.py:357
  88.8 3.3 %copy-start.14 = (f32[32,1152]{1,0:T(8,128)}, f32[32,1152]{1,0:T(8,128)S(1)}, u32[]{:S(2)}) copy-start(f32[32,1152]{1,0:T(8,128)S(1)} %collective-permute-done.21.refs_3_) | copy-start | bytes 442372
  88.9 13.0 %collective-permute-start.14 = (f32[32,1024]{1,0:T(8,128)S(1)}, f32[32,1024]{1,0:T(8,128)S(1)}, u32[]{:S(2)}, u32[]{:S(2)}) collective-permute-start(f32[32,1024]{1,0:T(8,128)S(1)} %get-tuple-element.44), channel_id=1, source_target_pairs={{0,2},{1,3},{2,0},{3,1},{4,6},{5,7},{6,4},{7,5},{8,10},{9,11},{10,... | collective-permute-start | bytes 393224 | tf_op jit(solution)/shard_map/ppermute | solution.py:357
  90.1 2.0 %copy-start.15 = (f32[32,1152]{1,0:T(8,128)}, f32[32,1152]{1,0:T(8,128)S(1)}, u32[]{:S(2)}) copy-start(f32[32,1152]{1,0:T(8,128)S(1)} %collective-permute-done.20.refs_2_) | copy-start | bytes 442372
  90.1 11.8 %collective-permute-start.13 = (f32[32,1024]{1,0:T(8,128)S(1)}, f32[32,1024]{1,0:T(8,128)S(1)}, u32[]{:S(2)}, u32[]{:S(2)}) collective-permute-start(f32[32,1024]{1,0:T(8,128)S(1)} %get-tuple-element.45.refs_0_), channel_id=1, source_target_pairs={{0,1},{1,0},{2,3},{3,2},{4,5},{5,4},{6,7},{7,6},{8,9},{9,8},{10,11... | collective-permute-start | bytes 393224 | tf_op jit(solution)/shard_map/ppermute | solution.py:357
  92.1 0.7 copy-start.6
  101.8 0.8 copy-start.8
  101.8 0.8 copy-start.16
  101.9 0.8 copy-start.17
  101.9 0.9 copy-start.18

commit v2 on v0

v2 whole, which is shorter than its diff:
```python
import functools

import jax
import jax.numpy as jnp
from jax import lax
from jax.experimental import pallas as pl
from jax.experimental.pallas import tpu as pltpu
from jax.sharding import PartitionSpec as P

F32, BF16 = jnp.float32, jnp.bfloat16
CHUNKS = 2
TILE = 512
LANES = 128
SUBLANES = 8
MIB = 1024 * 1024

IN_VMEM = pl.BlockSpec(memory_space=pltpu.VMEM)
IN_SMEM = pl.BlockSpec(memory_space=pltpu.SMEM)
ANYWHERE = pl.BlockSpec(memory_space=pl.ANY)


def split(value):
    high = value.astype(BF16)
    return high, (value - high.astype(F32)).astype(BF16)


def dot(a, b):
    return jnp.dot(a, b, preferred_element_type=F32)


def dot3(a, b):
    return dot(a[0], b[0]) + (dot(a[0], b[1]) + dot(a[1], b[0]))


def iota(shape, dim):
    return lax.broadcasted_iota(jnp.int32, shape, dim)


def low_bits(value, size):
    assert size & (size - 1) == 0
    return value & (size - 1)


def over(value, size):
    assert size & (size - 1) == 0
    return value >> (size.bit_length() - 1)


def pick(index, values):
    out = jnp.zeros(index.shape, values[0].dtype)
    for at, value in enumerate(values):
        out = jnp.where(index == at, value, out)
    return out


def tiles(width):
    step = min(TILE, width)
    return [(at, min(step, width - at)) for at in range(0, width, step)]


def slice_weights(dims, sign, order_ref, table_ref, rows_ref):
    per, groups, zb, cells = dims
    ang = lax.axis_index("ang")
    for d in range(groups):
        group = lax.rem(ang + sign * d + groups, groups)
        for z in range(zb):
            for a in range(per):
                at = (d * zb + z) * per + a
                rows_ref[at:at + 1, :] = table_ref[pl.ds(order_ref[group * per + a], 1), :]
    wide = rows_ref[...]
    total = wide.shape[1]
    row_slice = low_bits(over(iota(wide.shape, 0), per), zb)
    lane_slice = over(iota(wide.shape, 1), cells)
    out = jnp.zeros_like(wide)
    for z in range(zb):
        shift = lax.rem(z * cells - ang * cells + total, total)
        here = jnp.logical_and(row_slice == z, lane_slice == z)
        out = jnp.where(here, pltpu.roll(wide, shift, 1), out)
    return out


def volume_pieces(dims, zdev, half, offset, width):
    odd = lax.rem(lax.axis_index("slab"), 2)
    zb = dims[2]
    for h in range(2):
        start = lax.rem(odd + h, 2) * half + offset
        for zp in range(zdev // zb):
            yield h, zp, slice(zp * zb, (zp + 1) * zb), pl.ds(pl.multiple_of(start, LANES), width)


def rays_kernel(dims, first, half, offset, width, *refs):
    per, groups, zb, cells = dims
    count = groups * SUBLANES
    if first:
        order_ref, start_ref, len_ref, table_ref, vol_ref, *refs = refs
    else:
        given_ref, vol_ref, *refs = refs
    outs, refs = refs[:2 * groups], refs[2 * groups:]
    if first:
        left_ref, base_ref, buf, sems, table_buf, rows_ref, table_sem = refs
    else:
        buf, sems = refs
    zdev = vol_ref.shape[0]
    copies = {}
    if first:
        table_copy = pltpu.make_async_copy(table_ref, table_buf, table_sem)
        table_copy.start()
    for h, zp, slices, columns in volume_pieces(dims, zdev, half, offset, width):
        copies[h, zp] = pltpu.make_async_copy(
            vol_ref.at[slices, :, columns], buf.at[h, slices], sems.at[h, zp]
        )
        copies[h, zp].start()
    if first:
        shape = (zdev * per, LANES)
        angle, lane = low_bits(iota(shape, 0), per), iota(shape, 1)
        starts = pick(angle, [start_ref[0, a].astype(F32) for a in range(per)])
        lengths = pick(angle, [len_ref[0, a].astype(F32) for a in range(per)])
        foot = jnp.where(lane == 0, starts, jnp.where(lane == 1, lengths, 0.0))
        for h in range(2):
            for d in range(groups):
                outs[h * groups + d][:, width:] = foot if d == 0 else jnp.zeros_like(foot)
        table_copy.wait()
        both = jnp.concatenate(split(slice_weights(dims, 1, order_ref, table_buf, rows_ref)), axis=0)
        left = jnp.concatenate([both, both], axis=1)
        left_ref[...] = left
        base_ref[...] = slice_weights(dims, -1, order_ref, table_buf, rows_ref)
    else:
        left = given_ref[...]
    for (h, zp), copy in copies.items():
        copy.wait()
        for at, size in tiles(width):
            columns = slice(at, at + size)
            parts = [split(buf[h, zp * zb + z, :, columns]) for z in range(zb)]
            product = dot(left, jnp.concatenate([p[0] for p in parts] + [p[1] for p in parts], axis=0))
            sums = product[:count] + product[count:]
            for d in range(groups):
                outs[h * groups + d][zp * SUBLANES:(zp + 1) * SUBLANES, columns] = (
                    sums[d * SUBLANES:(d + 1) * SUBLANES]
                )


def ray_sums(dims, chunk, offset, width, given, small, table, volume):
    per, groups, zb, cells = dims
    zdev, _, total = volume.shape
    first = chunk == 0
    count, all_cells = groups * SUBLANES, table.shape[1]
    out = jax.ShapeDtypeStruct((zdev * per, width + (LANES if first else 0)), F32)
    left = jax.ShapeDtypeStruct((2 * count, 2 * zb * cells), BF16)
    base = jax.ShapeDtypeStruct((count, all_cells), F32)
    assert zb * cells == all_cells
    scratch = [pltpu.VMEM((2, zdev, cells, width), F32), pltpu.SemaphoreType.DMA((2, zdev // zb))]
    if first:
        scratch += [pltpu.VMEM(table.shape, F32), pltpu.VMEM(base.shape, F32), pltpu.SemaphoreType.DMA]
        args, specs = [*small, table, volume], [IN_SMEM] * 3 + [ANYWHERE, ANYWHERE]
        shapes = [out] * (2 * groups) + [left, base]
    else:
        args, specs = [given, volume], [IN_VMEM, ANYWHERE]
        shapes = [out] * (2 * groups)
    size = zdev * cells * width * 2
    return pl.pallas_call(
        functools.partial(rays_kernel, dims, first, total // 2, offset, width),
        in_specs=specs,
        out_specs=[IN_VMEM] * len(shapes),
        out_shape=shapes,
        scratch_shapes=scratch,
        compiler_params=pltpu.CompilerParams(vmem_limit_bytes=(58 if first else 50) * MIB),
        cost_estimate=pl.CostEstimate(flops=2 * size * 16, bytes_accessed=size * 4, transcendentals=0),
        name=f"ray_sums_{chunk}",
    )(*args)


def footprint_matrix(dims, zdev, rdev, foot):
    per, groups, zb, cells = dims
    block = zdev * per
    count, rows = 6 * block, 2 * per * rdev
    slab = lax.axis_index("slab")
    sibling = slab + 1 - 2 * lax.rem(slab, 2)
    start, length = foot[:, 0:1], foot[:, 1:2]
    at = low_bits(iota((count, 1), 0), block)
    slice_at = over(at, zb * per) * zb + low_bits(over(at, per), zb)
    span = jnp.where(length > 0.0, length, 1.0) / zdev
    centre = start + (slice_at.astype(F32) + 0.5) * span
    row_id = iota((1, rows), 1)
    row_slab = jnp.where(row_id < per * rdev, slab, sibling)
    row = (row_slab * rdev + low_bits(row_id, rdev)).astype(F32)
    shape = (count, rows)
    same_angle = low_bits(iota(shape, 0), per) == low_bits(over(iota(shape, 1), rdev), per)
    hat = jnp.maximum(0.0, 1.0 - jnp.abs(row + 0.5 - centre) / span)
    inside = jnp.logical_and(row >= start, row < start + length)
    return jnp.where(jnp.logical_and(same_angle, inside), hat, 0.0)


def residual_kernel(dims, first, half, rdev, zdev, offset, width, *refs):
    per, groups, zb, cells = dims
    block = zdev * per
    if first:
        order_ref, table_ref, *refs = refs
    else:
        mats, inverse_ref, refs = refs[:4], refs[4], refs[5:]
    sums_refs, (mine_ref, theirs_ref), refs = refs[:3], refs[3:5], refs[5:]
    mine_out, sent_out, *refs = refs
    outs, refs = refs[:3], refs[3:]
    if first:
        foot = jnp.concatenate([r[i, :, width:] for r in sums_refs for i in range(2)], axis=0)
        kernel = footprint_matrix(dims, zdev, rdev, foot)
        count, rows = kernel.shape
        weight = jnp.broadcast_to(jnp.sum(kernel, axis=1, keepdims=True), (count, LANES))
        for i, ref in enumerate(outs):
            for j in range(2):
                ref[j, :, width:] = weight[(2 * i + j) * block:(2 * i + j + 1) * block]
        kernel_t = kernel.T
        cover = jnp.sum(kernel_t, axis=1, keepdims=True)
        angle = low_bits(over(iota((rows, 1), 0), rdev), per)
        path = jnp.zeros((rows, 1), F32)
        for a in range(per):
            at = order_ref[lax.axis_index("ang") * per + a]
            path = jnp.where(angle == a, jnp.sum(table_ref[pl.ds(at, 1), :], axis=1, keepdims=True), path)
        inverse = 1.0 / jnp.maximum(path * cover, 0.25)
        ahead, back = split(kernel_t), split(kernel)
        for ref, value in zip(refs, (*ahead, *back)):
            ref[...] = value
        refs[4][...] = jnp.broadcast_to(inverse, (rows, LANES))
    else:
        ahead, back = (mats[0][...], mats[1][...]), (mats[2][...], mats[3][...])
        inverse = inverse_ref[:, 0:1]
    start = lax.rem(lax.axis_index("slab"), 2) * half + offset
    for at, size in tiles(width):
        columns = slice(at, at + size)
        mine = mine_ref[:, :, pl.ds(pl.multiple_of(start + at, LANES), size)].astype(F32)
        theirs = theirs_ref[:, :, offset + at:offset + at + size]
        measured = jnp.concatenate([m.reshape(per * rdev, size) for m in (mine, theirs)], axis=0)
        sums = jnp.concatenate([r[i, :, columns] for r in sums_refs for i in range(2)], axis=0)
        residual = (measured - dot3(ahead, split(sums))) * inverse
        mine_out[:, :, columns] = residual[:per * rdev].reshape(per, rdev, size)
        sent_out[:, :, columns] = residual[per * rdev:].reshape(per, rdev, size)
        given = dot3(back, split(residual))
        for i, ref in enumerate(outs):
            for j in range(2):
                ref[j, :, columns] = given[(2 * i + j) * block:(2 * i + j + 1) * block]


def residual_step(dims, zdev, chunk, offset, width, mats, order, table, sums, measured, theirs):
    per, groups, zb, cells = dims
    _, rdev, total = measured.shape
    first = chunk == 0
    block = zdev * per
    count, rows = 6 * block, 2 * per * rdev
    given = jax.ShapeDtypeStruct((2, block, width + (LANES if first else 0)), F32)
    piece = jax.ShapeDtypeStruct((per, rdev, width), F32)
    shapes = [piece, piece, given, given, given]
    if first:
        args, specs = [order, table], [IN_SMEM, IN_VMEM]
        ahead, back = jax.ShapeDtypeStruct((rows, count), BF16), jax.ShapeDtypeStruct((count, rows), BF16)
        shapes += [ahead, ahead, back, back, jax.ShapeDtypeStruct((rows, LANES), F32)]
    else:
        args, specs = list(mats), [IN_VMEM] * len(mats)
    args += [*sums, measured, theirs]
    specs += [IN_VMEM] * 5
    return pl.pallas_call(
        functools.partial(residual_kernel, dims, first, total // 2, rdev, zdev, offset, width),
        in_specs=specs,
        out_specs=[IN_VMEM] * len(shapes),
        out_shape=shapes,
        compiler_params=pltpu.CompilerParams(vmem_limit_bytes=16 * MIB),
        cost_estimate=pl.CostEstimate(
            flops=12 * count * rows * width, bytes_accessed=8 * width * (count + rows), transcendentals=0
        ),
        name=f"residual_{chunk}",
    )(*args)


def update_kernel(dims, first, half, offset, width, depth, *refs):
    per, groups, zb, cells = dims
    count = groups * SUBLANES
    left_in, backs, refs = refs[0], refs[1:1 + 2 * groups], refs[1 + 2 * groups:]
    mine_ref, theirs_ref, vol_ref, *refs = refs
    if not first:
        refs = refs[2:]
    out_ref, res_ref, *refs = refs
    if first:
        left_out, *refs = refs
    buf, in_sems, out_sems, res_sems = refs
    zdev = vol_ref.shape[0]
    odd = lax.rem(lax.axis_index("slab"), 2)
    arrive, leave = {}, {}
    pieces = list(volume_pieces(dims, zdev, half, offset, width))
    for h, zp, slices, columns in pieces:
        arrive[h, zp] = pltpu.make_async_copy(
            vol_ref.at[slices, :, columns], buf.at[h, slices], in_sems.at[h, zp]
        )
        arrive[h, zp].start()
        leave[h, zp] = pltpu.make_async_copy(
            buf.at[h, slices], out_ref.at[slices, :, columns], out_sems.at[h, zp]
        )
    kept = []
    for h, ref in enumerate((mine_ref, theirs_ref)):
        start = pl.multiple_of(lax.rem(odd + h, 2) * half + offset, LANES)
        kept.append(pltpu.make_async_copy(ref, res_ref.at[:, :, pl.ds(start, width)], res_sems.at[h]))
        kept[h].start()
    if first:
        weights = left_in[...]
        pad = jnp.zeros((depth - 3 * count, weights.shape[1]), F32)
        lefts = left_out
        for zp in range(zdev // zb):
            rows = slice(zp * SUBLANES, (zp + 1) * SUBLANES)
            slices = jnp.concatenate([ref[rows, width:width + 1] for ref in backs[:groups]], axis=0)
            scaled = weights / jnp.sum(weights * slices, axis=0, keepdims=True)
            high = scaled.astype(BF16).astype(F32)
            stacked = jnp.concatenate([high, high, scaled - high, pad], axis=0)
            left_out[zp] = stacked.T.astype(BF16)
    else:
        lefts = left_in
    for h, zp, _, _ in pieces:
        rows = slice(zp * SUBLANES, (zp + 1) * SUBLANES)
        arrive[h, zp].wait()
        left = lefts[zp]
        for at, size in tiles(width):
            columns = slice(at, at + size)
            back = jnp.concatenate([backs[h * groups + d][rows, columns] for d in range(groups)], axis=0)
            high, low = split(back)
            pad = jnp.zeros((depth - 3 * count, size), BF16)
            change = dot(left, jnp.concatenate([high, low, high, pad], axis=0))
            for z in range(zb):
                buf[h, zp * zb + z, :, columns] += change[z * cells:(z + 1) * cells]
        leave[h, zp].start()
    for copy in kept + list(leave.values()):
        copy.wait()


def update_step(dims, chunk, offset, width, left, backs, mine, theirs, volume, out, res):
    per, groups, zb, cells = dims
    zdev, _, total = volume.shape
    first = chunk == 0
    count = groups * SUBLANES
    depth = -(-3 * count // LANES) * LANES
    args = [left, *backs, mine, theirs, volume]
    specs = [IN_VMEM] * (3 + len(backs)) + [ANYWHERE]
    shapes = [jax.ShapeDtypeStruct(volume.shape, F32), jax.ShapeDtypeStruct((*mine.shape[:2], total), F32)]
    aliases = {}
    if first:
        shapes.append(jax.ShapeDtypeStruct((zdev // zb, zb * cells, depth), BF16))
    else:
        aliases = {len(args): 0, len(args) + 1: 1}
        args += [out, res]
        specs += [ANYWHERE, ANYWHERE]
    size = zdev * cells * width * 2
    return pl.pallas_call(
        functools.partial(update_kernel, dims, first, total // 2, offset, width, depth),
        in_specs=specs,
        out_specs=[ANYWHERE, ANYWHERE] + [IN_VMEM] * (len(shapes) - 2),
        out_shape=shapes,
        scratch_shapes=[
            pltpu.VMEM((2, zdev, cells, width), F32),
            pltpu.SemaphoreType.DMA((2, zdev // zb)),
            pltpu.SemaphoreType.DMA((2, zdev // zb)),
            pltpu.SemaphoreType.DMA((2,)),
        ],
        input_output_aliases=aliases,
        compiler_params=pltpu.CompilerParams(vmem_limit_bytes=50 * MIB),
        cost_estimate=pl.CostEstimate(flops=2 * size * 48, bytes_accessed=size * 8, transcendentals=0),
        name=f"update_{chunk}",
    )(*args)


def body(volume, measured, foot_start, foot_len, order, table):
    slabs, groups = lax.axis_size("slab"), lax.axis_size("ang")
    per, rdev, total = measured.shape
    zdev, cells, _ = volume.shape
    half = total // 2
    zb = SUBLANES // per
    dims = (per, groups, zb, cells)
    base_width = half // CHUNKS
    widths = [base_width] * CHUNKS
    offsets = [sum(widths[:c]) for c in range(CHUNKS)]

    def along(value, to):
        pairs = [(s, to(s)) for s in range(slabs) if 0 <= to(s) < slabs]
        return lax.ppermute(value, "slab", pairs)

    def spread(value, other, d):
        if not (other or d):
            return value
        pairs = [
            (s * groups + a, (s ^ other) * groups + (a + d) % groups) for s in range(slabs) for a in range(groups)
        ]
        return lax.ppermute(value, ("slab", "ang"), pairs)

    def facing(s):
        return s ^ 2

    def beyond(s):
        return s - 4 if s & 2 else s + 4

    def back_from_beyond(s):
        return s + 4 if s & 2 else s - 4

    odd = lax.rem(lax.axis_index("slab"), 2)
    theirs = along(
        lax.dynamic_slice_in_dim(measured, (1 - odd) * half, half, 2).astype(F32), lambda s: s ^ 1
    )

    sums, left, base = [], None, None
    for c in range(CHUNKS):
        parts = ray_sums(
            dims, c, offsets[c], widths[c], left, (order, foot_start, foot_len), table, volume
        )
        if c == 0:
            left, base = parts[2 * groups:]
        parts = [spread(parts[h * groups + d], h, d) for h in range(2) for d in range(groups)]
        own = jnp.stack([sum(parts[:groups]), sum(parts[groups:])])
        near = along(own, facing)
        far = along(near, beyond)
        sums.append((own, near, far))
    pieces, given, mats = [], [], None
    for c in range(CHUNKS):
        mine, piece, own, near, far, *rest = residual_step(
            dims, zdev, c, offsets[c], widths[c], mats, order, table, sums[c], measured, theirs
        )
        mats = rest if c == 0 else mats
        pieces.append((mine, along(piece, lambda s: s ^ 1)))
        near = near + along(far, back_from_beyond)
        arrived = along(near, facing)
        halves = [own[i] + arrived[i] for i in range(2)]
        given.append([spread(halves[h], h, d) for h in range(2) for d in range(groups)])
    out, res, left = None, None, base
    for c in range(CHUNKS):
        out, res, *rest = update_step(
            dims, c, offsets[c], widths[c], left, given[c], *pieces[c], volume, out, res
        )
        left = rest[0] if c == 0 else left
    return out, res


def solution(mesh):
    return jax.shard_map(
        body,
        mesh=mesh,
        in_specs=(
            P("slab", "ang", None),
            P("ang", "slab", None),
            P("slab", "ang"),
            P("slab", "ang"),
            P(),
            P(),
        ),
        out_specs=(P("slab", "ang", None), P("ang", "slab", None)),
        check_vma=False,
    )
```

time: 423 us -> 88.1 us (0.21)
  waiting for transfers between devices: 199 us -> 27.6 us
  starting transfers between devices: 93.7 us -> 29.4 us
  matrix products: 58 us -> 0 us
  local copies, waits for them, and re-layouts: 46 us -> 0.78 us
  Pallas kernels: 0 us -> 28.1 us
  between operations: 14.3 us -> 0.95 us
  other arithmetic: 5.68 us -> 0.34 us
  blocking collectives: 4.55 us -> 0 us
    ppermute x12 -> x23, waiting for transfers between devices: 115 us -> 27.6 us  [the longest x11 24.8 us: along(): return lax.ppermute(value, 'slab', pairs)]
    ppermute x12 -> x23, starting transfers between devices: 93.6 us -> 29.4 us  [the longest x11 16.2 us: along(): return lax.ppermute(value, 'slab', pairs)]
    dot_general x6 -> x0, matrix products: 58 us -> none  [the longest x1 31.1 us: body(): update = jnp.einsum('ay,azx->zyx', weights_cells, back_all, precision=high)]
    psum x1 -> x0, waiting for transfers between devices: 42.6 us -> none  [body(): summed_all = lax.psum(ray_part, 'ang')]
    all_gather x1 -> x0, waiting for transfers between devices: 41.4 us -> none  [body(): lax.all_gather(back, 'ang', axis=0, tiled=True)]
    unnamed x22 -> x12, local copies, waits for them, and re-layouts: 41 us -> 0.78 us
    pallas_call x0 -> x6, Pallas kernels: none -> 28.1 us  [the longest x2 14.8 us: update_step(): pl.pallas_call(functools.partial(update_kernel, dims, first, total // 2,...]
    div x1 -> x0, other arithmetic: 5.14 us -> none  [body(): res_mine = (measured.astype(jnp.float32) - totals) / denom[:, :, None]]
  transfers between devices with their start and end apart: 14 -> 23, of which waited for: 9 -> 7; matrix products, arithmetic and copies ran while one was open for 5% -> 0% of each run, Pallas kernels for 0% -> 17%
where the time goes in v2:
time: 88.1 us; the launch traced here: 87.1 us
  starting transfers between devices  29.4 us (33%)
  Pallas kernels  28.1 us (32%)
  waiting for transfers between devices  27.6 us (31%)
  between operations  0.95 us (1%)
    ppermute x11, waiting for transfers between devices, along(): return lax.ppermute(value, 'slab', pairs)  24.8 us
    ppermute x11, starting transfers between devices, along(): return lax.ppermute(value, 'slab', pairs)  16.2 us
    pallas_call x2, Pallas kernels, update_step(): pl.pallas_call(functools.partial(update_kernel, dims, first, total // 2,...  14.8 us
    ppermute x12, starting transfers between devices, spread(): return lax.ppermute(value, ('slab', 'ang'), pairs)  13.2 us
    pallas_call x2, Pallas kernels, ray_sums(): pl.pallas_call(functools.partial(rays_kernel, dims, first, total // 2, of...  9.96 us
    pallas_call x2, Pallas kernels, residual_step(): pl.pallas_call(functools.partial(residual_kernel, dims, first, total // 2...  3.29 us
    ppermute x12, waiting for transfers between devices, spread(): return lax.ppermute(value, ('slab', 'ang'), pairs)  2.77 us
  transfers between devices with their start and end apart: 23, of which 7 were waited for; matrix products, arithmetic and copies ran while one was open for 0% of the time, Pallas kernels for 17%

profile of v2, /device:TPU:0, one launch (start us, length us, event | category | flops | bytes accessed | tf_op | source)
XLA Modules:
  0.0 87.1 jit_solution(11737681366892628515)
XLA Ops:
  0.6 0.0 copy-start.1
  0.6 0.0 copy-start.4
  0.7 0.0 copy-start
  0.7 6.2 %ray_sums_0.1 = (f32[32,1152]{1,0:T(8,128)}, f32[32,1152]{1,0:T(8,128)}, f32[32,1152]{1,0:T(8,128)}, f32[32,1152]{1,0:T(8,128)}, bf16[32,512]{1,0:T(8,128)(2,1)}, /*index=5*/f32[16,256]{1,0:T(8,128)}) custom-call(s32[64]{0:T(128)} %refs_0_.3, s32[1,4]{1,0:T(1,128)} %refs_1_.3, s32[1,4]{1,0:T(1,128)} %refs_2_.1, f32[64,256]{1,0:T(8,128)} %refs_1_.4, ...), custom_call_target="tpu_custom_call" | custom-call | flops 67108864 | bytes 8388608 | tf_op jit(solution)/shard_map/ray_sums_0/pallas_call | solution.py:160
  6.8 3.0 %collective-permute-start = (f32[32,1152]{1,0:T(8,128)}, f32[32,1152]{1,0:T(8,128)S(1)}, u32[]{:S(2)}, u32[]{:S(2)}) collective-permute-start(f32[32,1152]{1,0:T(8,128)} %get-tuple-element.32), channel_id=1, source_target_pairs={{0,1},{1,0},{2,3},{3,2},{4,5},{5,4},{6,7},{7,6},{8,9},{9,8},{10,11... | collective-permute-start | bytes 442376 | tf_op jit(solution)/shard_map/ppermute | solution.py:386
  9.9 0.0 collective-permute-start.1
  9.9 0.2 collective-permute-start.2
  10.1 0.0 copy-start.2
  10.1 0.8 copy-done.2
  10.8 0.0 copy-start.5
  10.8 3.8 %ray_sums_1.1 = (f32[32,1024]{1,0:T(8,128)S(1)}, f32[32,1024]{1,0:T(8,128)S(1)}, f32[32,1024]{1,0:T(8,128)S(1)}, f32[32,1024]{1,0:T(8,128)S(1)}) custom-call(bf16[32,512]{1,0:T(8,128)(2,1)S(1)} %copy-done.2, f32[8,128,4096]{2,1,0:T(8,128)} %refs_7_.3), custom_call_target="tpu_custom_call" | custom-call | flops 67108864 | bytes 8388608 | tf_op jit(solution)/shard_map/ray_sums_1/pallas_call | solution.py:160
  14.6 2.0 %collective-permute-start.12 = (f32[32,1024]{1,0:T(8,128)S(1)}, f32[32,1024]{1,0:T(8,128)S(1)}, u32[]{:S(2)}, u32[]{:S(2)}) collective-permute-start(f32[32,1024]{1,0:T(8,128)S(1)} %get-tuple-element.48), channel_id=1, source_target_pairs={{0,1},{1,0},{2,3},{3,2},{4,5},{5,4},{6,7},{7,6},{8,9},{9,8},{10,11... | collective-permute-start | bytes 393224 | tf_op jit(solution)/shard_map/ppermute | solution.py:386
  16.6 0.0 copy-done
  16.6 0.1 dynamic-slice_convert_fusion
  16.7 0.1 collective-permute-start.5
  16.8 0.0 collective-permute-done
  16.8 0.0 copy-done.5
  16.9 0.0 collective-permute-done.1
  16.9 0.0 collective-permute-done.2
  16.9 1.6 %collective-permute-start.3 = (f32[2,32,1152]{2,1,0:T(8,128)S(1)}, f32[2,32,1152]{2,1,0:T(8,128)S(1)}, u32[]{:S(2)}, u32[]{:S(2)}) collective-permute-start(f32[2,32,1152]{2,1,0:T(8,128)S(1)} %pad_maximum_fusion.refs_2_), channel_id=1, source_target_pairs={{0,4},{2,6},{4,0},{6,2},{8,12},{10,14},{12,8},{14,10},{16,20},{18,... | collective-permute-start | bytes 884744 | tf_op jit(solution)/shard_map/ppermute | solution.py:378
  18.5 0.2 collective-permute-start.13
  18.7 0.9 collective-permute-start.14
  19.6 0.8 collective-permute-done.12
  20.4 6.0 %collective-permute-done.3.refs_3_ = f32[2,32,1152]{2,1,0:T(8,128)S(1)} collective-permute-done((f32[2,32,1152]{2,1,0:T(8,128)S(1)}, f32[2,32,1152]{2,1,0:T(8,128)S(1)}, u32[]{:S(2)}, u32[]{:S(2)}) %collective-permute-start.3) | collective-permute-done | bytes 294944 | tf_op jit(solution)/shard_map/ppermute | solution.py:378
  26.4 3.5 %collective-permute-start.4 = (f32[2,32,1152]{2,1,0:T(8,128)S(1)}, f32[2,32,1152]{2,1,0:T(8,128)S(1)}, u32[]{:S(2)}, u32[]{:S(2)}) collective-permute-start(f32[2,32,1152]{2,1,0:T(8,128)S(1)} %collective-permute-done.3.refs_3_), channel_id=1, source_target_pairs={{0,8},{2,10},{8,16},{10,18},{12,4},{14,6},{16,24},{18,26},{20,12},... | collective-permute-start | bytes 884744 | tf_op jit(solution)/shard_map/ppermute | solution.py:378
  29.9 0.0 collective-permute-done.13
  29.9 0.0 collective-permute-done.14
  30.0 0.1 collective-permute-start.15
  30.0 5.9 %collective-permute-done.4.refs_4_ = f32[2,32,1152]{2,1,0:T(8,128)S(1)} collective-permute-done((f32[2,32,1152]{2,1,0:T(8,128)S(1)}, f32[2,32,1152]{2,1,0:T(8,128)S(1)}, u32[]{:S(2)}, u32[]{:S(2)}) %collective-permute-start.4) | collective-permute-done | bytes 294944 | tf_op jit(solution)/shard_map/ppermute | solution.py:378
  36.0 0.0 collective-permute-done.5.refs_6_.refs_9_
  36.0 0.0 copy-done.1
  36.0 0.0 copy-done.4
  36.0 2.1 %residual_0.1 = (f32[4,32,1024]{2,1,0:T(8,128)S(1)}, f32[4,32,1024]{2,1,0:T(8,128)S(1)}, f32[2,32,1152]{2,1,0:T(8,128)S(1)}, f32[2,32,1152]{2,1,0:T(8,128)S(1)},...) custom-call(s32[64]{0:T(128)S(1)} %copy-done.4, ...), custom_call_target="tpu_custom_call" | custom-call | flops 603979776 | bytes 3670016 | tf_op jit(solution)/shard_map/residual_0/pallas_call | solution.py:259
  38.1 1.3 %collective-permute-start.6 = (f32[2,32,1152]{2,1,0:T(8,128)S(1)}, f32[2,32,1152]{2,1,0:T(8,128)S(1)}, u32[]{:S(2)}, u32[]{:S(2)}) collective-permute-start(f32[2,32,1152]{2,1,0:T(8,128)S(1)} %get-tuple-element.37), channel_id=1, source_target_pairs={{4,12},{6,14},{8,0},{10,2},{12,20},{14,22},{16,8},{18,10},{20,28},... | collective-permute-start | bytes 884744 | tf_op jit(solution)/shard_map/ppermute | solution.py:378
  39.4 0.0 collective-permute-done.15.refs_6_
  39.4 5.0 %collective-permute-start.16 = (f32[2,32,1024]{2,1,0:T(8,128)S(1)}, f32[2,32,1024]{2,1,0:T(8,128)S(1)}, u32[]{:S(2)}, u32[]{:S(2)}) collective-permute-start(f32[2,32,1024]{2,1,0:T(8,128)S(1)} %collective-permute-done.15.refs_6_), channel_id=1, source_target_pairs={{0,8},{2,10},{8,16},{10,18},{12,4},{14,6},{16,24},{18,26},{20,12},... | collective-permute-start | bytes 786440 | tf_op jit(solution)/shard_map/ppermute | solution.py:378
  44.4 4.0 %collective-permute-done.6 = f32[2,32,1152]{2,1,0:T(8,128)S(1)} collective-permute-done((f32[2,32,1152]{2,1,0:T(8,128)S(1)}, f32[2,32,1152]{2,1,0:T(8,128)S(1)}, u32[]{:S(2)}, u32[]{:S(2)}) %collective-permute-start.6) | collective-permute-done | bytes 294944 | tf_op jit(solution)/shard_map/ppermute | solution.py:378
  48.5 0.8 collective-permute-start.7
  49.3 0.0 collective-permute-done.16.refs_7_
  49.3 1.2 %residual_1.1 = (f32[4,32,1024]{2,1,0:T(8,128)S(1)}, f32[4,32,1024]{2,1,0:T(8,128)S(1)}, f32[2,32,1024]{2,1,0:T(8,128)S(1)}, f32[2,32,1024]{2,1,0:T(8,128)S(1)}, f32[2,32,1024]{2,1,0:T(8,128)S(1)}) custom-call(bf16[256,192]{1,0:T(8,128)(2,1)S(1)} %get-tuple-element.41.refs_0_, bf16[256,192]{1,0:T(8,128)(2,1)S(1)} %get-tuple-element.42.refs_1_, ...), custom_call_target="tpu_custom_call" | custom-call | flops 603979776 | bytes 3670016 | tf_op jit(solution)/shard_map/residual_1/pallas_call | solution.py:259
  50.5 1.3 %collective-permute-start.17 = (f32[2,32,1024]{2,1,0:T(8,128)S(1)}, f32[2,32,1024]{2,1,0:T(8,128)S(1)}, u32[]{:S(2)}, u32[]{:S(2)}) collective-permute-start(f32[2,32,1024]{2,1,0:T(8,128)S(1)} %get-tuple-element.53), channel_id=1, source_target_pairs={{4,12},{6,14},{8,0},{10,2},{12,20},{14,22},{16,8},{18,10},{20,28},... | collective-permute-start | bytes 786440 | tf_op jit(solution)/shard_map/ppermute | solution.py:378
  51.8 0.1 collective-permute-start.22
  51.9 0.5 collective-permute-start.11
  52.4 6.9 %collective-permute-done.17 = f32[2,32,1024]{2,1,0:T(8,128)S(1)} collective-permute-done((f32[2,32,1024]{2,1,0:T(8,128)S(1)}, f32[2,32,1024]{2,1,0:T(8,128)S(1)}, u32[]{:S(2)}, u32[]{:S(2)}) %collective-permute-start.17) | collective-permute-done | bytes 262176 | tf_op jit(solution)/shard_map/ppermute | solution.py:378
  59.3 2.0 %collective-permute-start.18 = (f32[2,32,1024]{2,1,0:T(8,128)S(1)}, f32[2,32,1024]{2,1,0:T(8,128)S(1)}, u32[]{:S(2)}, u32[]{:S(2)}) collective-permute-start(f32[2,32,1024]{2,1,0:T(8,128)S(1)} %add.53), channel_id=1, source_target_pairs={{0,4},{2,6},{4,0},{6,2},{8,12},{10,14},{12,8},{14,10},{16,20},{18,... | collective-permute-start | bytes 786440 | tf_op jit(solution)/shard_map/ppermute | solution.py:378
  61.3 0.0 collective-permute-done.7
  61.3 0.1 collective-permute-start.10
  61.4 2.3 %collective-permute-start.9 = (f32[32,1152]{1,0:T(8,128)S(1)}, f32[32,1152]{1,0:T(8,128)S(1)}, u32[]{:S(2)}, u32[]{:S(2)}) collective-permute-start(f32[32,1152]{1,0:T(8,128)S(1)} %get-tuple-element.58), channel_id=1, source_target_pairs={{0,2},{1,3},{2,0},{3,1},{4,6},{5,7},{6,4},{7,5},{8,10},{9,11},{10,... | collective-permute-start | bytes 442376 | tf_op jit(solution)/shard_map/ppermute | solution.py:386
  63.7 2.1 %collective-permute-done.18 = f32[2,32,1024]{2,1,0:T(8,128)S(1)} collective-permute-done((f32[2,32,1024]{2,1,0:T(8,128)S(1)}, f32[2,32,1024]{2,1,0:T(8,128)S(1)}, u32[]{:S(2)}, u32[]{:S(2)}) %collective-permute-start.18) | collective-permute-done | bytes 262176 | tf_op jit(solution)/shard_map/ppermute | solution.py:378
  65.7 2.3 %collective-permute-start.8 = (f32[32,1152]{1,0:T(8,128)S(1)}, f32[32,1152]{1,0:T(8,128)S(1)}, u32[]{:S(2)}, u32[]{:S(2)}) collective-permute-start(f32[32,1152]{1,0:T(8,128)S(1)} %get-tuple-element.59.refs_1_), channel_id=1, source_target_pairs={{0,1},{1,0},{2,3},{3,2},{4,5},{5,4},{6,7},{7,6},{8,9},{9,8},{10,11... | collective-permute-start | bytes 442376 | tf_op jit(solution)/shard_map/ppermute | solution.py:386
  68.1 0.0 collective-permute-done.11.refs_6_
  68.1 0.1 collective-permute-start.21
  68.2 0.0 collective-permute-done.10.refs_4_
  68.2 0.1 collective-permute-start.20
  68.3 0.0 collective-permute-done.9.refs_3_
  68.3 2.0 %collective-permute-start.19 = (f32[32,1024]{1,0:T(8,128)S(1)}, f32[32,1024]{1,0:T(8,128)S(1)}, u32[]{:S(2)}, u32[]{:S(2)}) collective-permute-start(f32[32,1024]{1,0:T(8,128)S(1)} %get-tuple-element.61.refs_1_), channel_id=1, source_target_pairs={{0,1},{1,0},{2,3},{3,2},{4,5},{5,4},{6,7},{7,6},{8,9},{9,8},{10,11... | collective-permute-start | bytes 393224 | tf_op jit(solution)/shard_map/ppermute | solution.py:386
  70.3 1.9 %collective-permute-done.8.refs_2_ = f32[32,1152]{1,0:T(8,128)S(1)} collective-permute-done((f32[32,1152]{1,0:T(8,128)S(1)}, f32[32,1152]{1,0:T(8,128)S(1)}, u32[]{:S(2)}, u32[]{:S(2)}) %collective-permute-start.8) | collective-permute-done | bytes 147488 | tf_op jit(solution)/shard_map/ppermute | solution.py:386
  72.2 0.0 copy-done.3
  72.2 7.4 %update_0.1 = (f32[8,128,4096]{2,1,0:T(8,128)}, f32[4,32,4096]{2,1,0:T(8,128)}, bf16[4,256,128]{2,1,0:T(8,128)(2,1)S(1)}) custom-call(f32[16,256]{1,0:T(8,128)S(1)} %copy-done.3, f32[32,1152]{1,0:T(8,128)S(1)} %get-tuple-element.59.refs_1_, f32[32,1152]{1,0:T(8,128)S(1)} %collective-permute-done.8.refs_2_, f32[32,1152]{1,0:T(8,128)S(1)} %collective-permute-done.9.refs_3_, ...), custom_call_target="tpu_custom_call" | custom-call | flops 201326592 | bytes 16777216 | tf_op jit(solution)/shard_map/update_0/pallas_call | solution.py:347
  79.7 0.0 collective-permute-done.22.refs_6_
  79.7 0.0 collective-permute-done.21.refs_4_
  79.7 0.0 collective-permute-done.20.refs_3_
  79.7 0.0 collective-permute-done.19.refs_2_
  79.7 7.4 %update_1.1 = (f32[8,128,4096]{2,1,0:T(8,128)}, f32[4,32,4096]{2,1,0:T(8,128)}) custom-call(bf16[4,256,128]{2,1,0:T(8,128)(2,1)S(1)} %get-tuple-element.40.refs_0_, f32[32,1024]{1,0:T(8,128)S(1)} %get-tuple-element.61.refs_1_, f32[32,1024]{1,0:T(8,128)S(1)} %collective-permute-done.19.refs_2_, ...), custom_call_target="tpu_custom_call", output_to_operand_aliasing={{0}: (8, {}), {1}: (9, {})} | custom-call | flops 201326592 | bytes 16777216 | tf_op jit(solution)/shard_map/update_1/pallas_call | solution.py:347
  (11 shorter events, 0.2 us)
Async XLA Ops:
  0.6 35.4 %copy-start.1 = (f32[64,256]{1,0:T(8,128)S(1)}, f32[64,256]{1,0:T(8,128)}, u32[]{:S(2)}) copy-start(f32[64,256]{1,0:T(8,128)} %refs_1_.4) | copy-start | bytes 196612
  0.6 35.4 %copy-start.4 = (s32[64]{0:T(128)S(1)}, s32[64]{0:T(128)}, u32[]{:S(2)}) copy-start(s32[64]{0:T(128)} %refs_0_.3) | copy-start | bytes 772
  0.7 16.0 %copy-start = (bf16[4,32,4096]{2,1,0:T(8,128)(2,1)S(1)}, bf16[4,32,4096]{2,1,0:T(8,128)(2,1)}, u32[]{:S(2)}) copy-start(bf16[4,32,4096]{2,1,0:T(8,128)(2,1)} %refs_8_.1) | copy-start | bytes 3145732
  6.8 10.0 %collective-permute-start = (f32[32,1152]{1,0:T(8,128)}, f32[32,1152]{1,0:T(8,128)S(1)}, u32[]{:S(2)}, u32[]{:S(2)}) collective-permute-start(f32[32,1152]{1,0:T(8,128)} %get-tuple-element.32), channel_id=1, source_target_pairs={{0,1},{1,0},{2,3},{3,2},{4,5},{5,4},{6,7},{7,6},{8,9},{9,8},{10,11... | collective-permute-start | bytes 442376 | tf_op jit(solution)/shard_map/ppermute | solution.py:386
  9.9 7.0 %collective-permute-start.1 = (f32[32,1152]{1,0:T(8,128)}, f32[32,1152]{1,0:T(8,128)S(1)}, u32[]{:S(2)}, u32[]{:S(2)}) collective-permute-start(f32[32,1152]{1,0:T(8,128)} %get-tuple-element.33), channel_id=1, source_target_pairs={{0,2},{1,3},{2,0},{3,1},{4,6},{5,7},{6,4},{7,5},{8,10},{9,11},{10,... | collective-permute-start | bytes 442376 | tf_op jit(solution)/shard_map/ppermute | solution.py:386
  9.9 7.0 %collective-permute-start.2 = (f32[32,1152]{1,0:T(8,128)}, f32[32,1152]{1,0:T(8,128)S(1)}, u32[]{:S(2)}, u32[]{:S(2)}) collective-permute-start(f32[32,1152]{1,0:T(8,128)} %get-tuple-element.34), channel_id=1, source_target_pairs={{0,3},{1,2},{2,1},{3,0},{4,7},{5,6},{6,5},{7,4},{8,11},{9,10},{10,... | collective-permute-start | bytes 442376 | tf_op jit(solution)/shard_map/ppermute | solution.py:386
  10.1 0.8 copy-start.2
  10.8 6.0 %copy-start.5 = (f32[32,1152]{1,0:T(8,128)S(1)}, f32[32,1152]{1,0:T(8,128)}, u32[]{:S(2)}) copy-start(f32[32,1152]{1,0:T(8,128)} %get-tuple-element.31) | copy-start | bytes 442372
  10.8 61.4 %copy-start.3 = (f32[16,256]{1,0:T(8,128)S(1)}, f32[16,256]{1,0:T(8,128)}, u32[]{:S(2)}) copy-start(f32[16,256]{1,0:T(8,128)} %get-tuple-element.30.refs_0_) | copy-start | bytes 49156
  14.6 5.8 %collective-permute-start.12 = (f32[32,1024]{1,0:T(8,128)S(1)}, f32[32,1024]{1,0:T(8,128)S(1)}, u32[]{:S(2)}, u32[]{:S(2)}) collective-permute-start(f32[32,1024]{1,0:T(8,128)S(1)} %get-tuple-element.48), channel_id=1, source_target_pairs={{0,1},{1,0},{2,3},{3,2},{4,5},{5,4},{6,7},{7,6},{8,9},{9,8},{10,11... | collective-permute-start | bytes 393224 | tf_op jit(solution)/shard_map/ppermute | solution.py:386
  16.7 19.2 %collective-permute-start.5 = (f32[4,32,2048]{2,1,0:T(8,128)S(1)}, f32[4,32,2048]{2,1,0:T(8,128)S(1)}, u32[]{:S(2)}, u32[]{:S(2)}) collective-permute-start(f32[4,32,2048]{2,1,0:T(8,128)S(1)} %dynamic-slice_convert_fusion), channel_id=1, source_target_pairs={{0,2},{2,0},{4,6},{6,4},{8,10},{10,8},{12,14},{14,12},{16,18},{18,... | collective-permute-start | bytes 3145736 | tf_op jit(solution)/shard_map/ppermute | solution.py:378
  16.9 9.5 %collective-permute-start.3 = (f32[2,32,1152]{2,1,0:T(8,128)S(1)}, f32[2,32,1152]{2,1,0:T(8,128)S(1)}, u32[]{:S(2)}, u32[]{:S(2)}) collective-permute-start(f32[2,32,1152]{2,1,0:T(8,128)S(1)} %pad_maximum_fusion.refs_2_), channel_id=1, source_target_pairs={{0,4},{2,6},{4,0},{6,2},{8,12},{10,14},{12,8},{14,10},{16,20},{18,... | collective-permute-start | bytes 884744 | tf_op jit(solution)/shard_map/ppermute | solution.py:378
  18.5 11.4 %collective-permute-start.13 = (f32[32,1024]{1,0:T(8,128)S(1)}, f32[32,1024]{1,0:T(8,128)S(1)}, u32[]{:S(2)}, u32[]{:S(2)}) collective-permute-start(f32[32,1024]{1,0:T(8,128)S(1)} %get-tuple-element.49), channel_id=1, source_target_pairs={{0,2},{1,3},{2,0},{3,1},{4,6},{5,7},{6,4},{7,5},{8,10},{9,11},{10,... | collective-permute-start | bytes 393224 | tf_op jit(solution)/shard_map/ppermute | solution.py:386
  18.7 11.2 %collective-permute-start.14 = (f32[32,1024]{1,0:T(8,128)S(1)}, f32[32,1024]{1,0:T(8,128)S(1)}, u32[]{:S(2)}, u32[]{:S(2)}) collective-permute-start(f32[32,1024]{1,0:T(8,128)S(1)} %get-tuple-element.50), channel_id=1, source_target_pairs={{0,3},{1,2},{2,1},{3,0},{4,7},{5,6},{6,5},{7,4},{8,11},{9,10},{10,... | collective-permute-start | bytes 393224 | tf_op jit(solution)/shard_map/ppermute | solution.py:386
  26.4 9.6 %collective-permute-start.4 = (f32[2,32,1152]{2,1,0:T(8,128)S(1)}, f32[2,32,1152]{2,1,0:T(8,128)S(1)}, u32[]{:S(2)}, u32[]{:S(2)}) collective-permute-start(f32[2,32,1152]{2,1,0:T(8,128)S(1)} %collective-permute-done.3.refs_3_), channel_id=1, source_target_pairs={{0,8},{2,10},{8,16},{10,18},{12,4},{14,6},{16,24},{18,26},{20,12},... | collective-permute-start | bytes 884744 | tf_op jit(solution)/shard_map/ppermute | solution.py:378
  30.0 9.4 %collective-permute-start.15 = (f32[2,32,1024]{2,1,0:T(8,128)S(1)}, f32[2,32,1024]{2,1,0:T(8,128)S(1)}, u32[]{:S(2)}, u32[]{:S(2)}) collective-permute-start(f32[2,32,1024]{2,1,0:T(8,128)S(1)} %pad_maximum_fusion.1.refs_5_), channel_id=1, source_target_pairs={{0,4},{2,6},{4,0},{6,2},{8,12},{10,14},{12,8},{14,10},{16,20},{18,... | collective-permute-start | bytes 786440 | tf_op jit(solution)/shard_map/ppermute | solution.py:378
  38.1 10.4 %collective-permute-start.6 = (f32[2,32,1152]{2,1,0:T(8,128)S(1)}, f32[2,32,1152]{2,1,0:T(8,128)S(1)}, u32[]{:S(2)}, u32[]{:S(2)}) collective-permute-start(f32[2,32,1152]{2,1,0:T(8,128)S(1)} %get-tuple-element.37), channel_id=1, source_target_pairs={{4,12},{6,14},{8,0},{10,2},{12,20},{14,22},{16,8},{18,10},{20,28},... | collective-permute-start | bytes 884744 | tf_op jit(solution)/shard_map/ppermute | solution.py:378
  39.4 9.9 %collective-permute-start.16 = (f32[2,32,1024]{2,1,0:T(8,128)S(1)}, f32[2,32,1024]{2,1,0:T(8,128)S(1)}, u32[]{:S(2)}, u32[]{:S(2)}) collective-permute-start(f32[2,32,1024]{2,1,0:T(8,128)S(1)} %collective-permute-done.15.refs_6_), channel_id=1, source_target_pairs={{0,8},{2,10},{8,16},{10,18},{12,4},{14,6},{16,24},{18,26},{20,12},... | collective-permute-start | bytes 786440 | tf_op jit(solution)/shard_map/ppermute | solution.py:378
  48.5 12.8 %collective-permute-start.7 = (f32[2,32,1152]{2,1,0:T(8,128)S(1)}, f32[2,32,1152]{2,1,0:T(8,128)S(1)}, u32[]{:S(2)}, u32[]{:S(2)}) collective-permute-start(f32[2,32,1152]{2,1,0:T(8,128)S(1)} %add.46), channel_id=1, source_target_pairs={{0,4},{2,6},{4,0},{6,2},{8,12},{10,14},{12,8},{14,10},{16,20},{18,... | collective-permute-start | bytes 884744 | tf_op jit(solution)/shard_map/ppermute | solution.py:378
  50.5 8.7 %collective-permute-start.17 = (f32[2,32,1024]{2,1,0:T(8,128)S(1)}, f32[2,32,1024]{2,1,0:T(8,128)S(1)}, u32[]{:S(2)}, u32[]{:S(2)}) collective-permute-start(f32[2,32,1024]{2,1,0:T(8,128)S(1)} %get-tuple-element.53), channel_id=1, source_target_pairs={{4,12},{6,14},{8,0},{10,2},{12,20},{14,22},{16,8},{18,10},{20,28},... | collective-permute-start | bytes 786440 | tf_op jit(solution)/shard_map/ppermute | solution.py:378
  51.8 27.8 %collective-permute-start.22 = (f32[4,32,1024]{2,1,0:T(8,128)S(1)}, f32[4,32,1024]{2,1,0:T(8,128)S(1)}, u32[]{:S(2)}, u32[]{:S(2)}) collective-permute-start(f32[4,32,1024]{2,1,0:T(8,128)S(1)} %get-tuple-element.55), channel_id=1, source_target_pairs={{0,2},{2,0},{4,6},{6,4},{8,10},{10,8},{12,14},{14,12},{16,18},{18,... | collective-permute-start | bytes 1572872 | tf_op jit(solution)/shard_map/ppermute | solution.py:378
  51.9 16.2 %collective-permute-start.11 = (f32[4,32,1024]{2,1,0:T(8,128)S(1)}, f32[4,32,1024]{2,1,0:T(8,128)S(1)}, u32[]{:S(2)}, u32[]{:S(2)}) collective-permute-start(f32[4,32,1024]{2,1,0:T(8,128)S(1)} %get-tuple-element.39), channel_id=1, source_target_pairs={{0,2},{2,0},{4,6},{6,4},{8,10},{10,8},{12,14},{14,12},{16,18},{18,... | collective-permute-start | bytes 1572872 | tf_op jit(solution)/shard_map/ppermute | solution.py:378
  59.3 6.4 %collective-permute-start.18 = (f32[2,32,1024]{2,1,0:T(8,128)S(1)}, f32[2,32,1024]{2,1,0:T(8,128)S(1)}, u32[]{:S(2)}, u32[]{:S(2)}) collective-permute-start(f32[2,32,1024]{2,1,0:T(8,128)S(1)} %add.53), channel_id=1, source_target_pairs={{0,4},{2,6},{4,0},{6,2},{8,12},{10,14},{12,8},{14,10},{16,20},{18,... | collective-permute-start | bytes 786440 | tf_op jit(solution)/shard_map/ppermute | solution.py:378
  61.3 6.9 %collective-permute-start.10 = (f32[32,1152]{1,0:T(8,128)S(1)}, f32[32,1152]{1,0:T(8,128)S(1)}, u32[]{:S(2)}, u32[]{:S(2)}) collective-permute-start(f32[32,1152]{1,0:T(8,128)S(1)} %get-tuple-element.58), channel_id=1, source_target_pairs={{0,3},{1,2},{2,1},{3,0},{4,7},{5,6},{6,5},{7,4},{8,11},{9,10},{10,... | collective-permute-start | bytes 442376 | tf_op jit(solution)/shard_map/ppermute | solution.py:386
  61.4 6.9 %collective-permute-start.9 = (f32[32,1152]{1,0:T(8,128)S(1)}, f32[32,1152]{1,0:T(8,128)S(1)}, u32[]{:S(2)}, u32[]{:S(2)}) collective-permute-start(f32[32,1152]{1,0:T(8,128)S(1)} %get-tuple-element.58), channel_id=1, source_target_pairs={{0,2},{1,3},{2,0},{3,1},{4,6},{5,7},{6,4},{7,5},{8,10},{9,11},{10,... | collective-permute-start | bytes 442376 | tf_op jit(solution)/shard_map/ppermute | solution.py:386
  65.7 6.5 %collective-permute-start.8 = (f32[32,1152]{1,0:T(8,128)S(1)}, f32[32,1152]{1,0:T(8,128)S(1)}, u32[]{:S(2)}, u32[]{:S(2)}) collective-permute-start(f32[32,1152]{1,0:T(8,128)S(1)} %get-tuple-element.59.refs_1_), channel_id=1, source_target_pairs={{0,1},{1,0},{2,3},{3,2},{4,5},{5,4},{6,7},{7,6},{8,9},{9,8},{10,11... | collective-permute-start | bytes 442376 | tf_op jit(solution)/shard_map/ppermute | solution.py:386
  68.1 11.6 %collective-permute-start.21 = (f32[32,1024]{1,0:T(8,128)S(1)}, f32[32,1024]{1,0:T(8,128)S(1)}, u32[]{:S(2)}, u32[]{:S(2)}) collective-permute-start(f32[32,1024]{1,0:T(8,128)S(1)} %get-tuple-element.60), channel_id=1, source_target_pairs={{0,3},{1,2},{2,1},{3,0},{4,7},{5,6},{6,5},{7,4},{8,11},{9,10},{10,... | collective-permute-start | bytes 393224 | tf_op jit(solution)/shard_map/ppermute | solution.py:386
  68.2 11.5 %collective-permute-start.20 = (f32[32,1024]{1,0:T(8,128)S(1)}, f32[32,1024]{1,0:T(8,128)S(1)}, u32[]{:S(2)}, u32[]{:S(2)}) collective-permute-start(f32[32,1024]{1,0:T(8,128)S(1)} %get-tuple-element.60), channel_id=1, source_target_pairs={{0,2},{1,3},{2,0},{3,1},{4,6},{5,7},{6,4},{7,5},{8,10},{9,11},{10,... | collective-permute-start | bytes 393224 | tf_op jit(solution)/shard_map/ppermute | solution.py:386
  68.3 11.4 %collective-permute-start.19 = (f32[32,1024]{1,0:T(8,128)S(1)}, f32[32,1024]{1,0:T(8,128)S(1)}, u32[]{:S(2)}, u32[]{:S(2)}) collective-permute-start(f32[32,1024]{1,0:T(8,128)S(1)} %get-tuple-element.61.refs_1_), channel_id=1, source_target_pairs={{0,1},{1,0},{2,3},{3,2},{4,5},{5,4},{6,7},{7,6},{8,9},{9,8},{10,11... | collective-permute-start | bytes 393224 | tf_op jit(solution)/shard_map/ppermute | solution.py:386
